TPU v7x, 32 devices: a whole 2x2x4 slice. The times are simulated.
32 devices in a mesh: seq: 8 (over z, x), dp: 4 (over y, core).
Axes of the slice: x: 2, y: 2, z: 4, core: 2. Of those that a mesh axis runs over, the one named last changes fastest.
Arguments:
- patches: bfloat16 [8, 4096, 4416], P('dp', 'seq'), may hold values from -6 to 6
- channel_mask: int32 [8, 69], P('dp'), may hold values 0 or 1
- lead_index: int32 [8], P('dp'), may hold values from 0 to 19
- patch_weight: float32 [4416, 768], P('seq'), may hold values from -0.09375 to 0.09375
- attention_weight: float32 [4, 768, 768], P(None, 'seq'), as said below
- forward_weight: float32 [2, 768, 3072], P(None, 'seq'), as said below
- vectors: float32 [25, 768], P(None, 'seq'), as said below
- patch_rows: float32 [4416], P('seq'), as said below
- patch_columns: float32 [768], replicated, as said below
- attention_rows: float32 [4, 768], P(None, 'seq'), as said below
- attention_columns: float32 [4, 768], replicated, as said below
- forward_rows: float32 [2, 768], P(None, 'seq'), as said below
- forward_columns: float32 [2, 3072], replicated, as said below
- vector_second: float32 [25, 768], P(None, 'seq'), as said below
- lead_average: float32 [20, 3], replicated, may hold values from 0.2 to 0.5
- output_cotangent: bfloat16 [8, 4096, 768], P('dp', 'seq'), may hold values from -6 to 6
- gate_cotangent: float32 [8, 3, 4096], P('dp', None, 'seq'), may hold values from -6 to 6
Outputs:
- block_output: bfloat16 [8, 4096, 768], P('dp', 'seq')
- expert_gates: float32 [8, 3, 4096], P('dp', None, 'seq')
- pixel_gradient: bfloat16 [8, 4096, 4416], P('dp', 'seq')
- patch_gradient: float32 [4416, 768], P('seq')
- attention_gradient: float32 [4, 768, 768], P(None, 'seq')
- forward_gradient: float32 [2, 768, 3072], P(None, 'seq')
- vector_gradient: float32 [25, 768], P(None, 'seq')
- patch_rows_new: float32 [4416], P('seq')
- patch_columns_new: float32 [768], replicated
- attention_rows_new: float32 [4, 768], P(None, 'seq')
- attention_columns_new: float32 [4, 768], replicated
- forward_rows_new: float32 [2, 768], P(None, 'seq')
- forward_columns_new: float32 [2, 3072], replicated
- vector_second_new: float32 [25, 768], P(None, 'seq')
- patch_weight_new: float32 [4416, 768], P('seq')
- attention_weight_new: float32 [4, 768, 768], P(None, 'seq')
- forward_weight_new: float32 [2, 768, 3072], P(None, 'seq')
- vectors_new: float32 [25, 768], P(None, 'seq')
- lead_stats: float32 [2, 20, 3], replicated
Inputs may be any that keep to these rules, and one draw needn't show every extreme that they name: `attention_weight`: independent normal entries, a scale for each slice. `forward_weight`: independent normal entries, a scale for each slice. `vectors`: gains near 1; head rows and lead embeddings independent normal. `patch_rows`: Positive. `patch_columns`: Positive. `attention_rows`: Positive. `attention_columns`: Positive. `forward_rows`: Positive. `forward_columns`: Positive. `vector_second`: Positive.
All inputs are finite; a program needn't handle non-finite values. No bound on the sum of `channel_mask` on one device may be relied on, other than what follows from the above.
Results may differ from a plain program's by a relative error of at most 0.015.
Values may be sent and summed in bfloat16 or wider, within the bound.
No kernel may reach another device: no remote copies, remote signals or barrier semaphores. Data moves between devices by JAX's collectives and lax.ppermute only.
A program may use at most 448 MiB of HBM per device.

v0:
```python
import jax
import jax.numpy as jnp
from jax import lax
from jax.sharding import PartitionSpec as P

H = 12
HD = 64
STEP = 10


norm_epsilon = 1e-06
square_floor = 1e-30
relative_rate = 1.0
clip_limit = 1.0
average_decay = 0.9
highest = lax.Precision.HIGHEST


def exact_gelu(values):
    return jax.nn.gelu(values, approximate=False)


def norm_forward(values, gain_row):
    center = jnp.mean(values, -1, keepdims=True)
    shifted = values - center
    variance = jnp.mean(shifted * shifted, -1, keepdims=True)
    inverse = lax.rsqrt(variance + norm_epsilon)
    standard = shifted * inverse
    return (standard * gain_row, standard, inverse)


def norm_backward(incoming, standard, inverse, gain_row):
    scaled_grad = incoming * gain_row
    first_mean = jnp.mean(scaled_grad, -1, keepdims=True)
    cross_mean = jnp.mean(scaled_grad * standard, -1, keepdims=True)
    return (
        inverse * (scaled_grad - first_mean - standard * cross_mean),
        jnp.sum(incoming * standard, (0, 1)),
    )


def head_slice(array_value, head):
    return lax.dynamic_slice_in_dim(array_value, head * HD, HD, array_value.ndim - 1)


def factor_parts(gradient, rows_old, master, decay_rate):
    square = gradient * gradient + square_floor
    rows_new = decay_rate * rows_old + (1.0 - decay_rate) * jnp.mean(square, -1)
    ratio_part = jnp.sum(gradient * gradient / rows_new[..., None], -2)
    return (
        rows_new,
        jnp.sum(square, -2),
        jnp.sum(rows_new, -1),
        jnp.sum(master * master, (-2, -1)),
        ratio_part,
    )


def factor_finish(
    gradient, rows_new, columns_old, column_total, rows_total, decay_rate, band_count
):
    row_count = gradient.shape[-2] * band_count
    columns_new = decay_rate * columns_old + (1.0 - decay_rate) * column_total / row_count
    mean_rows = rows_total / row_count
    estimate = rows_new[..., :, None] * columns_new[..., None, :] / mean_rows[..., None, None]
    return (columns_new, gradient * lax.rsqrt(estimate), mean_rows, row_count * gradient.shape[-1])


def factor_apply(master, update, mean_square, weight_total, element_count):
    shrink = jnp.maximum(1.0, jnp.sqrt(mean_square) / clip_limit)
    rate_value = relative_rate * jnp.sqrt(weight_total / element_count)
    return master - (rate_value / shrink)[..., None, None] * update


def local(
    patches,
    channel_mask,
    lead_index,
    patch_weight,
    attention_weight,
    forward_weight,
    vectors,
    patch_rows,
    patch_columns,
    attention_rows,
    attention_columns,
    forward_rows,
    forward_columns,
    vector_second,
    lead_average,
    output_cotangent,
    gate_cotangent,
):
    frames, frame_rows, patch_width = patches.shape
    channels = channel_mask.shape[1]
    band_count = lax.axis_size("seq")
    patch_full, attention_full, forward_full, vector_full = (
        lax.all_gather(patch_weight.astype(jnp.bfloat16), "seq", axis=0, tiled=True),
        lax.all_gather(attention_weight.astype(jnp.bfloat16), "seq", axis=1, tiled=True),
        lax.all_gather(forward_weight.astype(jnp.bfloat16), "seq", axis=1, tiled=True),
        lax.all_gather(vectors.astype(jnp.bfloat16), "seq", axis=1, tiled=True),
    )
    model_width = patch_full.shape[1]
    lead_count = vector_full.shape[0] - 5
    scale_value = HD ** (-0.5)
    head_numbers = jnp.arange(H, dtype=jnp.int32)
    mask_values = channel_mask.astype(jnp.bfloat16)
    masked = (
        patches.reshape(frames, frame_rows, channels, patch_width // channels)
        * mask_values[:, None, :, None]
    ).reshape(frames, frame_rows, patch_width)
    embedded = jnp.einsum("fsp,pd->fsd", masked, patch_full, preferred_element_type=jnp.float32)
    lead_hot = (lead_index[:, None] == jnp.arange(lead_count, dtype=jnp.int32)[None, :]).astype(
        jnp.float32
    )
    lead_rows = jnp.dot(lead_hot, vector_full[5:].astype(jnp.float32), precision=highest)
    residual_zero = embedded + lead_rows[:, None, :]
    gain_one = vector_full[0].astype(jnp.float32)
    gain_two = vector_full[1].astype(jnp.float32)
    head_rows = vector_full[2:5].astype(jnp.float32)
    normed_one, standard_one, inverse_one = norm_forward(residual_zero, gain_one)
    normed_one = normed_one.astype(jnp.bfloat16)
    projected = jnp.einsum(
        "fsd,kdn->kfsn", normed_one, attention_full[:3], preferred_element_type=jnp.float32
    ).astype(jnp.bfloat16)
    query = projected[0]
    full_kv = lax.all_gather(projected[1:], "seq", axis=2, tiled=True)

    def forward_head(head):
        query_head = head_slice(query, head)
        key_head = head_slice(full_kv[0], head)
        value_head = head_slice(full_kv[1], head)
        scores = (
            jnp.einsum("fqe,fke->fqk", query_head, key_head, preferred_element_type=jnp.float32)
            * scale_value
        )
        row_peak = jnp.max(scores, -1, keepdims=True)
        powered = jnp.exp(scores - row_peak)
        total = jnp.sum(powered, -1, keepdims=True)
        weights = (powered / total).astype(jnp.bfloat16)
        head_out = jnp.einsum(
            "fqk,fke->fqe", weights, value_head, preferred_element_type=jnp.float32
        ).astype(jnp.bfloat16)
        return (head_out, (row_peak + jnp.log(total))[..., 0])

    head_outs, log_totals = lax.map(forward_head, head_numbers)
    attended = jnp.moveaxis(head_outs, 0, 2).reshape(frames, frame_rows, model_width)
    residual_one = residual_zero + jnp.einsum(
        "fsn,nd->fsd", attended, attention_full[3], preferred_element_type=jnp.float32
    )
    normed_two, standard_two, inverse_two = norm_forward(residual_one, gain_two)
    normed_two = normed_two.astype(jnp.bfloat16)
    upward = jnp.einsum(
        "fsd,dh->fsh", normed_two, forward_full[0], preferred_element_type=jnp.float32
    )
    hidden, gelu_pull = jax.vjp(exact_gelu, upward)
    hidden = hidden.astype(jnp.bfloat16)
    residual_two = residual_one + jnp.einsum(
        "fsh,dh->fsd", hidden, forward_full[1], preferred_element_type=jnp.float32
    )
    logits = jnp.einsum("fsd,ed->fes", residual_two, head_rows, precision=highest)
    expert_gates = jax.nn.softmax(logits, axis=1)
    logit_grad = expert_gates * (
        gate_cotangent - jnp.sum(expert_gates * gate_cotangent, 1, keepdims=True)
    )
    adjoint_two = output_cotangent.astype(jnp.float32) + jnp.einsum(
        "fes,ed->fsd", logit_grad, head_rows, precision=highest
    )
    head_gradient = jnp.einsum("fes,fsd->ed", logit_grad, residual_two, precision=highest)
    adjoint_two_low = adjoint_two.astype(jnp.bfloat16)
    down_term = jnp.einsum(
        "fsd,fsh->dh", adjoint_two_low, hidden, preferred_element_type=jnp.float32
    )
    hidden_grad = jnp.einsum(
        "fsd,dh->fsh", adjoint_two_low, forward_full[1], preferred_element_type=jnp.float32
    )
    upward_grad = gelu_pull(hidden_grad)[0].astype(jnp.bfloat16)
    upward_term = jnp.einsum(
        "fsd,fsh->dh", normed_two, upward_grad, preferred_element_type=jnp.float32
    )
    normed_two_grad = jnp.einsum(
        "fsh,dh->fsd", upward_grad, forward_full[0], preferred_element_type=jnp.float32
    )
    through_two, gain_two_grad = norm_backward(normed_two_grad, standard_two, inverse_two, gain_two)
    adjoint_one = adjoint_two + through_two
    adjoint_one_low = adjoint_one.astype(jnp.bfloat16)
    output_term = jnp.einsum(
        "fsn,fsd->nd", attended, adjoint_one_low, preferred_element_type=jnp.float32
    )
    attended_grad = jnp.einsum(
        "fsd,nd->fsn", adjoint_one_low, attention_full[3], preferred_element_type=jnp.float32
    ).astype(jnp.bfloat16)

    def joint_head(head):
        query_head = head_slice(query, head)
        key_head = head_slice(full_kv[0], head)
        value_head = head_slice(full_kv[1], head)
        outgrad_head = head_slice(attended_grad, head)
        scores = (
            jnp.einsum("fqe,fke->fqk", query_head, key_head, preferred_element_type=jnp.float32)
            * scale_value
        )
        probability = jnp.exp(scores - log_totals[head][..., None])
        prob_grad = jnp.einsum(
            "fqe,fke->fqk", outgrad_head, value_head, preferred_element_type=jnp.float32
        )
        row_dot = jnp.sum(probability * prob_grad, -1, keepdims=True)
        score_grad = (probability * (prob_grad - row_dot)).astype(jnp.bfloat16)
        query_grad = (
            jnp.einsum("fqk,fke->fqe", score_grad, key_head, preferred_element_type=jnp.float32)
            * scale_value
        ).astype(jnp.bfloat16)
        key_grad = (
            jnp.einsum("fqk,fqe->fke", score_grad, query_head, preferred_element_type=jnp.float32)
            * scale_value
        )
        value_grad = jnp.einsum(
            "fqk,fqe->fke",
            probability.astype(jnp.bfloat16),
            outgrad_head,
            preferred_element_type=jnp.float32,
        )
        return (query_grad, jnp.stack([key_grad, value_grad], 0))

    query_grads, kv_terms = lax.map(joint_head, head_numbers)
    kv_parts = lax.psum_scatter(kv_terms, "seq", scatter_dimension=3, tiled=True)
    query_grad_rows = jnp.moveaxis(query_grads, 0, 2).reshape(frames, frame_rows, model_width)
    kv_grads = (
        jnp.transpose(kv_parts, (1, 2, 3, 0, 4))
        .reshape(2, frames, frame_rows, model_width)
        .astype(jnp.bfloat16)
    )
    head_grads = jnp.concatenate([query_grad_rows[None], kv_grads], 0)
    projection_term = jnp.einsum(
        "fsd,kfsn->kdn", normed_one, head_grads, preferred_element_type=jnp.float32
    )
    normed_one_grad = jnp.einsum(
        "kfsn,kdn->fsd", head_grads, attention_full[:3], preferred_element_type=jnp.float32
    )
    through_one, gain_one_grad = norm_backward(normed_one_grad, standard_one, inverse_one, gain_one)
    adjoint_zero = adjoint_one + through_one
    adjoint_zero_low = adjoint_zero.astype(jnp.bfloat16)
    patch_term = jnp.einsum(
        "fsp,fsd->pd", masked, adjoint_zero_low, preferred_element_type=jnp.float32
    )
    pixel_term = jnp.einsum(
        "fsd,pd->fsp", adjoint_zero_low, patch_full, preferred_element_type=jnp.float32
    )
    pixel_gradient = (
        (
            pixel_term.reshape(frames, frame_rows, channels, -1)
            * mask_values.astype(jnp.float32)[:, None, :, None]
        )
        .reshape(frames, frame_rows, patch_width)
        .astype(jnp.bfloat16)
    )
    lead_term = jnp.dot(lead_hot.T, jnp.sum(adjoint_zero, 1), precision=highest)
    vector_term = jnp.concatenate(
        [gain_one_grad[None], gain_two_grad[None], head_gradient, lead_term], 0
    )
    attention_term = jnp.concatenate([projection_term, output_term[None]], 0)
    forward_term = jnp.stack([upward_term, down_term])
    gate_frames = jnp.sum(expert_gates, 2)
    lead_sums = jnp.dot(lead_hot.T, gate_frames, precision=highest)
    lead_counts = jnp.sum(lead_hot, 0) * frame_rows
    vector_total, lead_sums, lead_counts = lax.psum(
        (vector_term, lead_sums, lead_counts), ("seq", "dp")
    )
    band_sums = (
        lax.psum_scatter(patch_term, "seq", scatter_dimension=0, tiled=True),
        lax.psum_scatter(attention_term, "seq", scatter_dimension=1, tiled=True),
        lax.psum_scatter(forward_term, "seq", scatter_dimension=1, tiled=True),
    )
    patch_gradient, attention_gradient, forward_gradient = (
        lax.psum(band_sums[0].astype(jnp.bfloat16), "dp").astype(jnp.float32),
        lax.psum(band_sums[1].astype(jnp.bfloat16), "dp").astype(jnp.float32),
        lax.psum(band_sums[2].astype(jnp.bfloat16), "dp").astype(jnp.float32),
    )
    vector_columns = vectors.shape[1]
    vector_gradient = lax.dynamic_slice_in_dim(
        vector_total, lax.axis_index("seq") * vector_columns, vector_columns, 1
    )
    decay_rate = 1.0 - STEP ** (-0.8)
    gradients = [patch_gradient, attention_gradient, forward_gradient]
    masters = [patch_weight, attention_weight, forward_weight]
    column_olds = [patch_columns, attention_columns, forward_columns]
    prepared = [
        factor_parts(patch_gradient, patch_rows, patch_weight, decay_rate),
        factor_parts(attention_gradient, attention_rows, attention_weight, decay_rate),
        factor_parts(forward_gradient, forward_rows, forward_weight, decay_rate),
    ]
    vector_second_new = decay_rate * vector_second + (1.0 - decay_rate) * (
        vector_gradient * vector_gradient + square_floor
    )
    vector_update = vector_gradient * lax.rsqrt(vector_second_new)
    vector_squares = jnp.sum(vector_update * vector_update, -1)
    vector_sizes = jnp.sum(vectors * vectors, -1)
    summed = lax.psum(
        (
            prepared[0][1],
            prepared[1][1],
            prepared[2][1],
            prepared[0][2],
            prepared[1][2],
            prepared[2][2],
            prepared[0][3],
            prepared[1][3],
            prepared[2][3],
            vector_squares,
            vector_sizes,
        ),
        "seq",
    )
    finished = [
        factor_finish(
            gradients[number],
            prepared[number][0],
            column_olds[number],
            summed[number],
            summed[number + 3],
            decay_rate,
            band_count,
        )
        for number in range(3)
    ]
    squares = lax.psum(
        (
            jnp.sum(finished[0][1] * finished[0][1], (-2, -1)),
            jnp.sum(finished[1][1] * finished[1][1], (-2, -1)),
            jnp.sum(finished[2][1] * finished[2][1], (-2, -1)),
        ),
        "seq",
    )
    mean_squares = [squares[number] / finished[number][3] for number in range(3)]
    masters_new = [
        factor_apply(
            masters[number],
            finished[number][1],
            mean_squares[number],
            summed[6 + number],
            finished[number][3],
        )
        for number in range(3)
    ]
    full_width = vector_columns * band_count
    vector_shrink = jnp.maximum(1.0, jnp.sqrt(summed[9] / full_width) / clip_limit)
    vector_rate = relative_rate * jnp.sqrt(summed[10] / full_width)
    vectors_new = vectors - (vector_rate / vector_shrink)[:, None] * vector_update
    batch_mean = jnp.where(
        lead_counts[:, None] > 0, lead_sums / jnp.maximum(lead_counts, 1.0)[:, None], lead_average
    )
    new_average = average_decay * lead_average + (1.0 - average_decay) * batch_mean
    lead_stats = jnp.stack([new_average, new_average / (1.0 - average_decay**STEP)])
    block_output = residual_two.astype(jnp.bfloat16)
    return (
        block_output,
        expert_gates,
        pixel_gradient,
        patch_gradient,
        attention_gradient,
        forward_gradient,
        vector_gradient,
        prepared[0][0],
        finished[0][0],
        prepared[1][0],
        finished[1][0],
        prepared[2][0],
        finished[2][0],
        vector_second_new,
        masters_new[0],
        masters_new[1],
        masters_new[2],
        vectors_new,
        lead_stats,
    )


def solution(mesh):
    return jax.shard_map(
        local,
        mesh=mesh,
        in_specs=(
            P("dp", "seq", None),
            P("dp", None),
            P("dp"),
            P("seq", None),
            P(None, "seq", None),
            P(None, "seq", None),
            P(None, "seq"),
            P("seq"),
            P(),
            P(None, "seq"),
            P(),
            P(None, "seq"),
            P(),
            P(None, "seq"),
            P(),
            P("dp", "seq", None),
            P("dp", None, "seq"),
        ),
        out_specs=(
            P("dp", "seq", None),
            P("dp", None, "seq"),
            P("dp", "seq", None),
            P("seq", None),
            P(None, "seq", None),
            P(None, "seq", None),
            P(None, "seq"),
            P("seq"),
            P(),
            P(None, "seq"),
            P(),
            P(None, "seq"),
            P(),
            P(None, "seq"),
            P("seq", None),
            P(None, "seq", None),
            P(None, "seq", None),
            P(None, "seq"),
            P(),
        ),
        check_vma=False,
    )
```

profile of v0, /device:TPU:0, one launch (start us, length us, event | category | flops | bytes accessed | tf_op | source)
XLA Modules:
  0.0 3887.4 jit_solution(2149118946839555115)
XLA Ops:
  13.8 32.8 all-gather
  47.6 72.1 %all-gather.6.cloned.1.call-done = bf16[4416,768]{1,0:T(8,128)(2,1)} async-done(((bf16[552,768]{1,0:T(8,128)(2,1)}), bf16[4416,768]{1,0:T(8,128)(2,1)}) %all-gather.6.cloned.1.call-update) | async-done | bytes 6782992 | tf_op jit(solution)/shard_map/all_gather | solution.py:98
  119.7 12.6 add_reduce_fusion
  132.9 67.6 %all-gather.8.cloned.1.call-done = bf16[4,768,768]{2,1,0:T(8,128)(2,1)} async-done(((bf16[4,96,768]{2,1,0:T(8,128)(2,1)}), bf16[4,768,768]{2,1,0:T(8,128)(2,1)}) %all-gather.8.cloned.1.call-update) | async-done | bytes 4718608 | tf_op jit(solution)/shard_map/all_gather | solution.py:99
  217.2 472.4 %all-gather.10.cloned.1.call-done = bf16[2,2,4096,768]{3,2,0,1:T(8,128)(2,1)} async-done(((bf16[2,2,512,768]{3,2,0,1:T(8,128)(2,1)}), bf16[2,2,4096,768]{3,2,0,1:T(8,128)(2,1)}) %all-gather.10.cloned.1.call-update) | async-done | bytes 25165840 | tf_op jit(solution)/shard_map/all_gather | solution.py:127
  689.6 31.0 copy.160
  720.8 479.1 %while.24 = (s32[]{:T(128)}, bf16[12,2,512,64]{2,3,0,1:T(8,128)(2,1)S(1)}, f32[12,2,512]{2,1,0:T(2,128)S(1)}, s32[12]{0:T(128)S(1)}, bf16[2,512,768]{1,2,0:T(8,1...) while((s32[]{:T(128)}, ...), condition=%wide.region_5.6_spmd, body=%wide.region_2.5_spmd.sunk | while | flops 1111555072 | bytes 103056568 | solution.py:146
  722.0 13.9 fusion.149
  763.0 13.8 fusion.149
  802.9 13.9 fusion.149
  842.8 13.8 fusion.149
  882.6 13.8 fusion.149
  922.4 13.8 fusion.149
  962.2 13.8 fusion.149
  1002.0 13.8 fusion.149
  1041.8 13.8 fusion.149
  1081.6 13.8 fusion.149
  1121.5 13.8 fusion.149
  1161.3 13.8 fusion.149
  1206.5 15.3 fusion.64
  1221.9 30.9 multiply_convert_fusion.2
  1268.0 17.2 add_convert_fusion
  1303.2 726.7 %while.25 = (s32[]{:T(128)}, bf16[12,2,512,64]{2,3,0,1:T(8,128)(2,1)S(1)}, f32[12,2,2,4096,64]{3,4,0,2,1:T(8,128)}, s32[12]{0:T(128)S(1)}, bf16[2,512,768]{1,2,0...) while((s32[]{:T(128)}, ...), condition=%wide.region_15.16_spmd, body=%wide.region_13.15_spmd.sunk | while | flops 2736389120 | bytes 276461824 | solution.py:225
  1306.4 13.8 fusion.160
  1341.6 11.0 multiply_convert_fusion.8
  1367.0 13.8 fusion.160
  1402.1 11.0 multiply_convert_fusion.8
  1427.4 13.8 fusion.160
  1487.9 13.8 fusion.160
  1548.5 13.8 fusion.160
  1609.0 13.8 fusion.160
  1669.6 13.8 fusion.160
  1730.2 13.8 fusion.160
  1790.7 13.8 fusion.160
  1851.3 13.8 fusion.160
  1911.9 13.8 fusion.160
  1972.5 13.8 fusion.160
  2055.5 768.3 %reduce-scatter.4.cloned.1.call-done = f32[12,2,2,512,64]{3,4,0,2,1:T(8,128)} async-done(((f32[12,2,2,4096,64]{3,4,0,2,1:T(8,128)}), f32[12,2,2,512,64]{3,4,0,2,1:T(8,128)}) %reduce-scatter.4.cloned.1.call-update) | async-done | bytes 6291472 | tf_op jit(solution)/shard_map/reduce_scatter | solution.py:226
  2841.4 12.9 convolution_bitcast_fusion
  2857.2 43.4 %all-reduce.1 = (f32[20,3]{0,1:T(4,128)S(1)}, f32[20]{0:T(128)S(1)}) all-reduce(f32[20,3]{0,1:T(4,128)S(1)} %fusion.93, f32[20]{0:T(128)S(1)} %broadcast_multiply_fusion.6), channel_id=1, replica_groups=mesh['seq'=8,'dp'=4] {'seq','dp'}, use_global_device_ids=true, to_apply=%region_63.64 | all-reduce | flops 80 | bytes 640 | tf_op jit(solution)/shard_map/psum | solution.py:266
  2907.3 234.2 %reduce-scatter.8.cloned.1.call-done = f32[2,96,3072]{2,1,0:T(8,128)} async-done(((f32[2,768,3072]{2,1,0:T(8,128)}), f32[2,96,3072]{2,1,0:T(8,128)}) %reduce-scatter.8.cloned.1.call-update) | async-done | bytes 2359312 | tf_op jit(solution)/shard_map/reduce_scatter | solution.py:272
  3155.4 12.2 copy.174
  3168.6 441.1 %all-reduce.12 = bf16[4,768,768]{2,0,1:T(4,128)(2,1)} all-reduce(f32[4,768,768]{2,0,1:T(4,128)} %copy.174), channel_id=4, replica_groups=mesh['seq'=8,'dp'=4] {'seq'}, use_global_device_ids=true, to_apply=%region_21.22.clone | all-reduce | flops 2359296 | bytes 14155776
  3614.4 12.8 multiply_convert_fusion.1
  3627.2 106.3 %all-reduce.9.cloned.1.call-done = f32[25,768]{1,0:T(8,128)} async-done(((f32[25,768]{1,0:T(8,128)}), f32[25,768]{1,0:T(8,128)}) %all-reduce.9.cloned.1.call-update) | async-done | bytes 76816 | tf_op jit(solution)/shard_map/psum | solution.py:266
  3734.4 64.1 %all-reduce.11.cloned.1.call-done = (bf16[4,96,768]{2,0,1:T(4,128)(2,1)}, bf16[552,768]{1,0:T(8,128)(2,1)}, bf16[2,96,3072]{2,1,0:T(8,128)(2,1)}) async-done(((bf16[4,96,768]{2,0,1:T(4,128)(2,1)}, bf16[552,768]{1,0:T(8,128)(2,1)}, bf16[2,96,3072]{2,1,0:T(8,128)(2,1)}), (bf16[4,96,768]{2,0,1:T(4,128)(2,1)}, bf16[552,768]{1,0:T(8,128)(2,1)}, bf16[2,96,3072]{2,1,0:T(8,128)(2,1)})) %all-reduce.11.cloned.1.call-update) | async-done | bytes 2617360 | tf_op jit(solution)/shard_map/psum | solution.py:276
  3807.2 38.6 all-reduce.3
  3851.2 17.8 all-reduce.2
  (499 shorter events, 972.2 us)
Async XLA Ops:
  7.2 40.2 %copy-start.82 = (s32[2]{0:T(128)S(1)}, s32[2]{0:T(128)}, u32[]{:S(2)}) copy-start(s32[2]{0:T(128)} %param.23) | copy-start | bytes 28
  7.2 112.4 %all-gather.6.cloned.1.call-start = ((), (), s32[]{:S(2)}) async-start(), calls=%async_computation.3 | async-start | bytes 7630848 | tf_op jit(solution)/shard_map/all_gather | solution.py:98
  11.2 189.3 %all-gather.8.cloned.1.call-start = ((), (), s32[]{:S(2)}) async-start(), calls=%async_computation.4 | async-start | bytes 5308416 | tf_op jit(solution)/shard_map/all_gather | solution.py:99
  12.8 676.7 %all-gather.10.cloned.1.call-start = ((), (), s32[]{:S(2)}) async-start(), calls=%async_computation.5 | async-start | bytes 28311552 | tf_op jit(solution)/shard_map/all_gather | solution.py:127
  13.1 119.2 %copy-start.60 = (bf16[2,4416]{1,0:T(2,128)(2,1)}, bf16[2,4416]{1,0:T(2,128)(2,1)S(1)}, u32[]{:S(2)}) copy-start(bf16[2,4416]{1,0:T(2,128)(2,1)S(1)} %mul.394) | copy-start | bytes 52996
  47.4 153.1 %copy-start.62 = (f32[768]{0:T(1024)}, f32[768]{0:T(1024)S(1)}, u32[]{:S(2)}) copy-start(f32[768]{0:T(1024)S(1)} %get-tuple-element.312) | copy-start | bytes 9220
  47.6 152.9 %copy-start.57 = (f32[2,768]{1,0:T(2,128)}, f32[2,768]{1,0:T(2,128)S(1)}, u32[]{:S(2)}) copy-start(f32[2,768]{1,0:T(2,128)S(1)} %fusion.84) | copy-start | bytes 18436
  132.3 74.5 %copy-start.11 = (f32[2,512,768]{2,1,0:T(8,128)}, f32[2,512,768]{2,1,0:T(8,128)S(1)}, u32[]{:S(2)}) copy-start(f32[2,512,768]{2,1,0:T(8,128)S(1)} %get-tuple-element.397) | copy-start | bytes 9437188
  132.3 74.5 %copy-start.50 = (f32[2,512]{1,0:T(2,128)}, f32[2,512]{1,0:T(2,128)S(1)}, u32[]{:S(2)}) copy-start(f32[2,512]{1,0:T(2,128)S(1)} %broadcast_multiply_fusion.5) | copy-start | bytes 12292
  132.9 73.9 %copy-start.64 = (f32[2,512]{1,0:T(2,128)}, f32[2,512]{1,0:T(2,128)S(1)}, u32[]{:S(2)}) copy-start(f32[2,512]{1,0:T(2,128)S(1)} %add_rsqrt_fusion.1) | copy-start | bytes 12292
  210.8 995.5 %all-gather.12.cloned.1.call-start = ((), (), s32[]{:S(2)}) async-start(), calls=%async_computation.6 | async-start | bytes 10616832 | tf_op jit(solution)/shard_map/all_gather | solution.py:100
  214.5 2609.3 %reduce-scatter.4.cloned.1.call-start = ((), (), s32[]{:S(2)}) async-start(), calls=%async_computation.7 | async-start | bytes 56623104 | tf_op jit(solution)/shard_map/reduce_scatter | solution.py:226
  720.8 480.7 %copy-start.58 = (f32[2,768]{1,0:T(2,128)S(1)}, f32[2,768]{1,0:T(2,128)}, u32[]{:S(2)}) copy-start(f32[2,768]{1,0:T(2,128)} %copy-done.57) | copy-start | bytes 18436
  1205.8 47.0 %copy-start.4 = (f32[2,512,768]{2,1,0:T(8,128)}, f32[2,512,768]{2,1,0:T(8,128)S(1)}, u32[]{:S(2)}) copy-start(f32[2,512,768]{2,1,0:T(8,128)S(1)} %get-tuple-element.399) | copy-start | bytes 9437188
  1205.8 89.9 %copy-start.42 = (f32[2,512]{1,0:T(2,128)}, f32[2,512]{1,0:T(2,128)S(1)}, u32[]{:S(2)}) copy-start(f32[2,512]{1,0:T(2,128)S(1)} %broadcast_multiply_fusion.4) | copy-start | bytes 12292
  1206.3 89.4 %copy-start.44 = (f32[2,512]{1,0:T(2,128)}, f32[2,512]{1,0:T(2,128)S(1)}, u32[]{:S(2)}) copy-start(f32[2,512]{1,0:T(2,128)S(1)} %add_rsqrt_fusion) | copy-start | bytes 12292
  1252.8 10.9 copy-start.6
  1252.8 10.8 copy-start.40
  1268.0 27.8 copy-start.2
  1285.2 10.6 copy-start.5
  2031.1 1110.4 %reduce-scatter.8.cloned.1.call-start = ((), (), s32[]{:S(2)}) async-start(), calls=%async_computation.9 | async-start | bytes 21233664 | tf_op jit(solution)/shard_map/reduce_scatter | solution.py:272
  2052.4 1559.5 %reduce-scatter.6.cloned.1.call-start = ((), (), s32[]{:S(2)}) async-start(), calls=%async_computation.8 | async-start | bytes 15261696 | tf_op jit(solution)/shard_map/reduce_scatter | solution.py:270
  2854.3 46.4 %copy-start.76 = (f32[20,3]{0,1:T(4,128)S(1)}, f32[20,3]{0,1:T(4,128)}, u32[]{:S(2)}) copy-start(f32[20,3]{0,1:T(4,128)} %param.35) | copy-start | bytes 724
  2854.3 47.0 %copy-start.72 = (f32[768]{0:T(1024)S(1)}, f32[768]{0:T(1024)}, u32[]{:S(2)}) copy-start(f32[768]{0:T(1024)} %get-tuple-element.301) | copy-start | bytes 9220
  2854.3 47.0 %copy-start.10 = (f32[2,512,768]{2,1,0:T(8,128)S(1)}, f32[2,512,768]{2,1,0:T(8,128)}, u32[]{:S(2)}) copy-start(f32[2,512,768]{2,1,0:T(8,128)} %copy-done.9) | copy-start | bytes 9437188
  2854.3 47.0 %copy-start.38 = (f32[2,3,512]{2,0,1:T(2,128)S(1)}, f32[2,3,512]{2,0,1:T(2,128)}, u32[]{:S(2)}) copy-start(f32[2,3,512]{2,0,1:T(2,128)} %param.37) | copy-start | bytes 36868
  2854.3 47.0 %copy-start.53 = (f32[2,512]{1,0:T(2,128)S(1)}, f32[2,512]{1,0:T(2,128)}, u32[]{:S(2)}) copy-start(f32[2,512]{1,0:T(2,128)} %copy-done.52) | copy-start | bytes 12292
  2854.4 879.1 %all-reduce.9.cloned.1.call-start = ((), (), s32[]{:S(2)}) async-start(), calls=%async_computation.10 | async-start | bytes 196608 | tf_op jit(solution)/shard_map/psum | solution.py:266
  2907.3 237.1 %copy-start.13 = (f32[2,512,768]{2,1,0:T(8,128)S(1)}, f32[2,512,768]{2,1,0:T(8,128)}, u32[]{:S(2)}) copy-start(f32[2,512,768]{2,1,0:T(8,128)} %copy-done.11) | copy-start | bytes 9437188
  3609.7 188.8 %all-reduce.11.cloned.1.call-start = ((), (), s32[]{:S(2)}) async-start(), calls=%async_computation.11 | async-start | bytes 5234688 | tf_op jit(solution)/shard_map/psum | solution.py:276
  3614.4 119.1 %copy-start.66 = (f32[25,96]{1,0:T(8,128)S(1)}, f32[25,96]{1,0:T(8,128)}, u32[]{:S(2)}) copy-start(f32[25,96]{1,0:T(8,128)} %param.34) | copy-start | bytes 28804
  3614.4 187.9 %copy-start.75 = (f32[4,96]{1,0:T(4,128)S(1)}, f32[4,96]{1,0:T(4,128)}, u32[]{:S(2)}) copy-start(f32[4,96]{1,0:T(4,128)} %param.30) | copy-start | bytes 4612
  3734.4 145.3 %copy-start.48 = (f32[25,96]{1,0:T(8,128)}, f32[25,96]{1,0:T(8,128)S(1)}, u32[]{:S(2)}) copy-start(f32[25,96]{1,0:T(8,128)S(1)} %get-tuple-element.365) | copy-start | bytes 28804
  3734.4 145.3 %copy-start.49 = (f32[25,96]{1,0:T(8,128)}, f32[25,96]{1,0:T(8,128)S(1)}, u32[]{:S(2)}) copy-start(f32[25,96]{1,0:T(8,128)S(1)} %get-tuple-element.366) | copy-start | bytes 28804
  3802.3 44.1 %copy-start.71 = (f32[768]{0:T(1024)S(1)}, f32[768]{0:T(1024)}, u32[]{:S(2)}) copy-start(f32[768]{0:T(1024)} %param.29) | copy-start | bytes 9220
  3802.3 44.2 %copy-start.67 = (f32[4,768]{1,0:T(4,128)S(1)}, f32[4,768]{1,0:T(4,128)}, u32[]{:S(2)}) copy-start(f32[4,768]{1,0:T(4,128)} %param.31) | copy-start | bytes 36868
  3802.5 44.0 %copy-start.69 = (f32[4,96]{1,0:T(4,128)}, f32[4,96]{1,0:T(4,128)S(1)}, u32[]{:S(2)}) copy-start(f32[4,96]{1,0:T(4,128)S(1)} %get-tuple-element.370) | copy-start | bytes 4612
  3802.5 44.1 %copy-start.56 = (f32[2,3072]{1,0:T(2,128)S(1)}, f32[2,3072]{1,0:T(2,128)}, u32[]{:S(2)}) copy-start(f32[2,3072]{1,0:T(2,128)} %param.33) | copy-start | bytes 73732
  3802.6 44.0 %copy-start.19 = (bf16[4,96,768]{2,0,1:T(4,128)(2,1)S(1)}, bf16[4,96,768]{2,0,1:T(4,128)(2,1)}, u32[]{:S(2)}) copy-start(bf16[4,96,768]{2,0,1:T(4,128)(2,1)} %get-tuple-element.359) | copy-start | bytes 1769476
  3806.3 71.3 %copy-start.8 = (f32[2,96,3072]{2,1,0:T(8,128)}, f32[2,96,3072]{2,1,0:T(8,128)S(1)}, u32[]{:S(2)}) copy-start(f32[2,96,3072]{2,1,0:T(8,128)S(1)} %get-tuple-element.373) | copy-start | bytes 7077892
  3806.3 44.9 %copy-start.77 = (f32[25]{0:T(128)S(1)}, f32[25]{0:T(128)}, u32[]{:S(2)}) copy-start(f32[25]{0:T(128)} %get-tuple-element.394) | copy-start | bytes 304
  3806.3 44.8 %copy-start.78 = (f32[4]{0:T(128)S(1)}, f32[4]{0:T(128)}, u32[]{:S(2)}) copy-start(f32[4]{0:T(128)} %get-tuple-element.392) | copy-start | bytes 52
  3806.3 44.8 %copy-start.79 = (f32[2]{0:T(128)S(1)}, f32[2]{0:T(128)}, u32[]{:S(2)}) copy-start(f32[2]{0:T(128)} %get-tuple-element.388) | copy-start | bytes 28
  3807.1 66.8 %copy-start.54 = (f32[552]{0:T(1024)}, f32[552]{0:T(1024)S(1)}, u32[]{:S(2)}) copy-start(f32[552]{0:T(1024)S(1)} %get-tuple-element.372) | copy-start | bytes 6628
  3807.2 70.4 %copy-start.68 = (f32[2,96]{1,0:T(2,128)}, f32[2,96]{1,0:T(2,128)S(1)}, u32[]{:S(2)}) copy-start(f32[2,96]{1,0:T(2,128)S(1)} %get-tuple-element.368) | copy-start | bytes 2308
  3846.5 27.4 copy-start.55
  3846.5 26.1 copy-start.41
  3846.6 31.1 copy-start.36
  (69 other events, 277.6 us)
Sparse Core Ops, SparseCore 0:
  11.3 108.3 all-gather.5
  122.4 78.0 all-gather.7
  211.0 478.5 all-gather.9
  692.2 138.0 all-gather.11
  2031.2 792.6 reduce-scatter.3
  2828.1 313.3 reduce-scatter.7
  3145.5 406.1 reduce-scatter.5
  3609.8 123.6 all-reduce.8
  3737.4 61.0 all-reduce.10
where the time goes:
time: 3900 us; the launch traced here: 3890 us
  waiting for transfers between devices  1790 us (46%)
  matrix products  647 us (17%)
  blocking collectives  574 us (15%)
  local copies, waits for them, and re-layouts  474 us (12%)
  other arithmetic  349 us (9%)
  loops' own time  39.8 us (1%)
    reduce_scatter x1, waiting for transfers between devices, local(): lax.psum_scatter(kv_terms, 'seq', scatter_dimension=3, tiled=True)  768 us
    all_gather x1, waiting for transfers between devices, local(): full_kv = lax.all_gather(projected[1:], 'seq', axis=2, tiled=True)  472 us
    unnamed x1, blocking collectives  441 us
    reduce_scatter x1, waiting for transfers between devices, local(): lax.psum_scatter(forward_term, 'seq', scatter_dimension=1, tiled=True)  234 us
    slice x12, local copies, waits for them, and re-layouts, forward_head(): value_head = head_slice(full_kv[1], head)  166 us
    slice x12, local copies, waits for them, and re-layouts, joint_head(): key_head = head_slice(full_kv[0], head)  166 us
    convert_element_type x12, other arithmetic, joint_head(): score_grad = (probability * (prob_grad - row_dot)).astype(jnp.bfloat16)  132 us
    dot_general x12, matrix products, joint_head(): jnp.einsum('fqe,fke->fqk', outgrad_head, value_head, preferred_element_ty...  112 us
  transfers between devices with their start and end apart: 9, of which 7 were waited for; matrix products, arithmetic and copies ran while one was open for 16% of the time, Pallas kernels for 0%

commit v1 on v0

v1 whole, which is shorter than its diff:
```python
import functools
import math

import jax
import jax.numpy as jnp
from jax import lax
from jax.experimental.layout import Layout, with_layout_constraint
from jax.experimental import pallas as pl
from jax.experimental.pallas import tpu as pltpu
from jax.sharding import Mesh, PartitionSpec as P

H = 12
HD = 64
STEP = 10
SEQ = ("ring", "band")

norm_epsilon = 1e-06
square_floor = 1e-30
relative_rate = 1.0
clip_limit = 1.0
average_decay = 0.9
highest = lax.Precision.HIGHEST
log2_e = math.log2(math.e)
vmem_limit = 56 * 1024 * 1024
ONES = 16


def gelu_pair(values):
    cumulative = 0.5 + 0.5 * lax.erf(values * math.sqrt(0.5))
    density = jnp.exp(-0.5 * values * values) * (1.0 / math.sqrt(2.0 * math.pi))
    return values * cumulative, cumulative + values * density


def norm_forward(values, gain_row):
    center = jnp.mean(values, -1, keepdims=True)
    shifted = values - center
    variance = jnp.mean(shifted * shifted, -1, keepdims=True)
    inverse = lax.rsqrt(variance + norm_epsilon)
    standard = shifted * inverse
    return (standard * gain_row, standard, inverse)


def norm_backward(incoming, standard, inverse, gain_row):
    scaled_grad = incoming * gain_row
    first_mean = jnp.mean(scaled_grad, -1, keepdims=True)
    cross_mean = jnp.mean(scaled_grad * standard, -1, keepdims=True)
    return (
        inverse * (scaled_grad - first_mean - standard * cross_mean),
        jnp.sum(incoming * standard, (0, 1)),
    )


def dot(left, right):
    return jnp.dot(left, right, preferred_element_type=jnp.float32)


def dot_rows(left, right):
    return lax.dot_general(
        left, right, (((1,), (1,)), ((), ())), preferred_element_type=jnp.float32
    )


def forward_kernel(q_ref, k_ref, v_ref, o_ref, lse_ref, key_rows, value_ones):
    chunks, width = k_ref.shape[0], k_ref.shape[3]

    @pl.when(pl.program_id(1) == 0)
    def _():
        for c in range(chunks):
            key_rows[c] = jnp.transpose(jnp.concatenate([k_ref[c, 0], k_ref[c, 0]], 0))
            value_ones[c, :HD] = v_ref[c, 0]
            value_ones[c, HD:] = jnp.ones((ONES, width), jnp.bfloat16)

    scaled = q_ref[0, 0].astype(jnp.float32) * log2_e
    first = scaled.astype(jnp.bfloat16)
    rest = (scaled - first.astype(jnp.float32)).astype(jnp.bfloat16)
    query = jnp.concatenate([first, rest], 0)
    peak = None
    coming = dot(key_rows[0], query)
    for c in range(chunks):
        scores = coming
        if c + 1 < chunks:
            coming = dot(key_rows[c + 1], query)
        if c == 1:
            total = dot(value_ones[0], powered)
        elif c > 1:
            total = total * shrink + dot(value_ones[c - 1], powered)
        chunk_peak = jnp.max(scores, 0, keepdims=True)
        higher = chunk_peak if c == 0 else jnp.maximum(peak, chunk_peak)
        powered = jnp.exp2(scores - higher).astype(jnp.bfloat16)
        if c > 0:
            shrink = jnp.exp2(peak - higher)
        peak = higher
    last = dot(value_ones[chunks - 1], powered)
    total = last if chunks == 1 else total * shrink + last
    weight_sum = total[HD : HD + 1]
    o_ref[0, 0] = (total[:HD] / weight_sum).astype(jnp.bfloat16)
    lse_ref[0, 0] = (peak + jnp.log2(weight_sum)) * (1.0 / log2_e)


def append_row(block, row):
    first = row.astype(jnp.bfloat16).astype(jnp.float32)
    rest = row - first
    second = rest.astype(jnp.bfloat16).astype(jnp.float32)
    third = rest - second
    place = lax.broadcasted_iota(jnp.int32, block.shape, 0)
    extra = jnp.where(
        place == 0, first, jnp.where(place == 1, second, jnp.where(place == 2, third, 0.0))
    )
    return jnp.concatenate([block, extra.astype(jnp.bfloat16)], 0)


def backward_kernel(
    q_ref, g_ref, o_ref, lse_ref, k_ref, v_ref, *refs, merged
):
    dq_ref, dkv_ref = (refs[0], refs[0]) if merged else refs[:2]
    key_rows, value_rows, sums = refs[-3:]
    chunks, width = k_ref.shape[0], k_ref.shape[3]
    step = pl.program_id(1)

    @pl.when(step == 0)
    def _():
        ones = jnp.ones((HD, width), jnp.bfloat16)
        for c in range(chunks):
            key_rows[c] = jnp.transpose(jnp.concatenate([k_ref[c, 0], ones], 0))
            value_rows[c] = jnp.transpose(jnp.concatenate([v_ref[c, 0], ones], 0))
            sums[c] = jnp.zeros((2 * HD, width), jnp.float32)

    query = q_ref[0, 0]
    outgrad = g_ref[0, 0]
    row_dot = jnp.sum(
        outgrad.astype(jnp.float32) * o_ref[0, 0].astype(jnp.float32), 0, keepdims=True
    )
    query_columns = append_row(query, -lse_ref[0, 0])
    outgrad_columns = append_row(outgrad, -row_dot)
    def accumulate(c, query_grad, score_grad, weights):
        sums[c, :HD] += dot_rows(query, score_grad)
        sums[c, HD:] += dot_rows(outgrad, weights)
        part = dot(k_ref[c, 0], score_grad)
        return part if query_grad is None else query_grad + part

    query_grad = None
    coming = dot(key_rows[0], query_columns), dot(value_rows[0], outgrad_columns)
    for c in range(chunks):
        scores, prob_grad = coming
        if c + 1 < chunks:
            coming = dot(key_rows[c + 1], query_columns), dot(value_rows[c + 1], outgrad_columns)
        if c > 0:
            query_grad = accumulate(c - 1, query_grad, score_grad, weights)
        probs = jnp.exp2(scores * log2_e)
        score_grad = (probs * prob_grad).astype(jnp.bfloat16)
        weights = probs.astype(jnp.bfloat16)
    query_grad = accumulate(chunks - 1, query_grad, score_grad, weights)
    if merged:
        dq_ref[step, 0] = query_grad.astype(jnp.bfloat16)
    else:
        dq_ref[0, 0] = query_grad.astype(jnp.bfloat16)
    slot = 1 if merged else 0

    @pl.when(step == pl.num_programs(1) - 1)
    def _():
        for c in range(chunks):
            dkv_ref[c, slot] = sums[c, :HD].astype(dkv_ref.dtype)
            dkv_ref[c, slot + 1] = sums[c, HD:].astype(dkv_ref.dtype)


def run_forward(received, before, start=0, count=None):
    query = join_chunks(received)
    if before:
        query = tie(query, *before)
    if lax.axis_size("ring") == 1:
        triple = tuple((query, kind) for kind in range(3))
    else:
        frame = lax.all_gather(query[:, 1:], "ring", axis=0, tiled=True)
        triple = ((query, 0), (frame, 0), (frame, 1))
    count = query.shape[0] - start if count is None else count
    here, totals = attention_forward(*triple, start, count)
    return triple, here, totals


def token_block(slot, width, start=0):
    return pl.BlockSpec((1, 1, HD, width), lambda head, step: (step + start, slot, head, 0))


def frame_block(slot, chunks, width):
    return pl.BlockSpec((chunks, 1, HD, width), lambda head, step: (0, slot, head, 0))


def lse_block(width):
    return pl.BlockSpec((1, 1, 1, width), lambda head, step: (head, step, 0, 0))


def kernel_cost(matmuls, heads, queries, keys, moved):
    return pl.CostEstimate(
        flops=2 * matmuls * heads * queries * keys * HD * 4,
        bytes_accessed=moved,
        transcendentals=heads * queries * keys,
    )


def attention_forward(query, key, value, start, count):
    (q_array, q_slot), (k_array, k_slot), (v_array, v_slot) = query, key, value
    lanes, width = q_array.shape[2:]
    q_chunks = count
    k_chunks = k_array.shape[0]
    heads = lanes // HD
    return pl.pallas_call(
        forward_kernel,
        grid=(heads, q_chunks),
        in_specs=[
            token_block(q_slot, width, start),
            frame_block(k_slot, k_chunks, width),
            frame_block(v_slot, k_chunks, width),
        ],
        out_specs=[token_block(0, width), lse_block(width)],
        out_shape=[
            jax.ShapeDtypeStruct((q_chunks, 1, lanes, width), jnp.bfloat16),
            jax.ShapeDtypeStruct((heads, q_chunks, 1, width), jnp.float32),
        ],
        scratch_shapes=[
            pltpu.VMEM((k_chunks, width, 2 * HD), jnp.bfloat16),
            pltpu.VMEM((k_chunks, HD + ONES, width), jnp.bfloat16),
        ],
        compiler_params=pltpu.CompilerParams(
            dimension_semantics=("arbitrary", "arbitrary"), vmem_limit_bytes=vmem_limit
        ),
        cost_estimate=kernel_cost(
            2, heads, q_chunks * width, k_chunks * width, 8 * lanes * width * (q_chunks + k_chunks)
        ),
        name="attention_forward",
    )(q_array, k_array, v_array)


def attention_backward(query, outgrad, attended, lse, key, value, merged):
    (q_array, q_slot), (k_array, k_slot), (v_array, v_slot) = query, key, value
    g_array, g_slot = outgrad
    q_chunks, _, lanes, width = q_array.shape
    k_chunks = k_array.shape[0]
    heads = lanes // HD
    if merged:
        out_specs = [pl.BlockSpec((k_chunks, 3, HD, width), lambda head, step: (0, 0, head, 0))]
        out_shape = [jax.ShapeDtypeStruct((k_chunks, 3, lanes, width), jnp.bfloat16)]
    else:
        out_specs = [
            token_block(0, width),
            pl.BlockSpec((k_chunks, 2, HD, width), lambda head, step: (0, 0, head, 0)),
        ]
        out_shape = [
            jax.ShapeDtypeStruct((q_chunks, 1, lanes, width), jnp.bfloat16),
            jax.ShapeDtypeStruct((k_chunks, 2, lanes, width), jnp.float32),
        ]
    return pl.pallas_call(
        functools.partial(backward_kernel, merged=merged),
        grid=(heads, q_chunks),
        in_specs=[
            token_block(q_slot, width),
            token_block(g_slot, width),
            token_block(0, width),
            lse_block(width),
            frame_block(k_slot, k_chunks, width),
            frame_block(v_slot, k_chunks, width),
        ],
        out_specs=out_specs,
        out_shape=out_shape,
        scratch_shapes=[
            pltpu.VMEM((k_chunks, width, 2 * HD), jnp.bfloat16),
            pltpu.VMEM((k_chunks, width, 2 * HD), jnp.bfloat16),
            pltpu.VMEM((k_chunks, 2 * HD, width), jnp.float32),
        ],
        compiler_params=pltpu.CompilerParams(
            dimension_semantics=("arbitrary", "arbitrary"), vmem_limit_bytes=vmem_limit
        ),
        cost_estimate=kernel_cost(
            5, heads, q_chunks * width, k_chunks * width, 16 * lanes * width * (q_chunks + k_chunks)
        ),
        name="attention_backward",
    )(q_array, g_array, attended, lse, k_array, v_array)


def exchange(parts):
    if parts.shape[0] == 1:
        return parts
    return lax.all_to_all(parts, "band", 0, 0, tiled=True)


def join_chunks(parts):
    if lax.axis_size("ring") == 1:
        return parts
    bands, slots, lanes, width = parts.shape
    return jnp.transpose(parts, (1, 2, 0, 3)).reshape(1, slots, lanes, bands * width)


def split_chunks(parts, bands):
    if lax.axis_size("ring") == 1:
        return parts
    _, slots, lanes, width = parts.shape
    return jnp.transpose(parts.reshape(slots, lanes, bands, width // bands), (2, 0, 1, 3))


def other_core(value):
    return lax.ppermute(value, "core", [(0, 1), (1, 0)])


def core_half(value, axis, own):
    axis = axis % value.ndim
    half = value.shape[axis] // 2
    place = lax.axis_index("core") * half
    return lax.dynamic_slice_in_dim(value, place if own else half - place, half, axis)


def swap_pairs(value):
    return lax.ppermute(value, "pair", [(0, 1), (1, 0)])


def doubling():
    count = lax.axis_size("band")
    return (
        lax.axis_size("ring") == 1
        and count >= 4
        and count & (count - 1) == 0
        and lax.axis_size("pair") == 2
    )


def swap_bands(value, step):
    return lax.ppermute(value, "band", [(i, i ^ step) for i in range(lax.axis_size("band"))])


def both(value, received, bit, axis):
    first = bit == 0
    return jnp.stack(
        [jnp.where(first, value, received), jnp.where(first, received, value)], axis
    )


def pair_half(shard):
    rows = shard.shape[0] // 2
    return lax.dynamic_slice_in_dim(shard, lax.axis_index("pair") * rows, rows, 0)


def join_pairs(rows, count):
    value = rows.reshape(count, -1, rows.shape[1])
    return both(value, swap_pairs(value), lax.axis_index("pair"), 1).reshape(
        2 * rows.shape[0], rows.shape[1]
    )


def ring_gather(block, *gates, both_cores=False, marks=None, passed=None, beside=None):
    gates = [*gates, *[()] * lax.axis_size("band")]
    count = lax.axis_size("band")
    middle = count // 2
    order = [2 * z for z in range(middle)] + [2 * z + 1 for z in reversed(range(middle))]
    onward = [(order[p], order[(p + 1) % count]) for p in range(count)]
    back = [(target, source) for source, target in onward]
    band, core = lax.axis_index("band"), lax.axis_index("core")
    place = jnp.where(band % 2 == 0, band // 2, count - 1 - band // 2)
    half = block.shape[1]

    def put(blocks, part, at, column=0):
        at = (at + count) % count
        source = jnp.where(at < middle, 2 * at, 2 * (count - 1 - at) + 1)
        if both_cores:
            other = other_core(part)
            blocks = lax.dynamic_update_slice(
                blocks, other[None], (source, 0, column + (1 - core) * half)
            )
            column = column + core * half
        return lax.dynamic_update_slice(blocks, part[None], (source, 0, column))

    columns = 2 * half if both_cores else half
    blocks = put(jnp.zeros((count, block.shape[0], columns), block.dtype), block, place)
    first = second = block
    for step in range(1, middle):
        first, second = lax.optimization_barrier((first, second, *gates[step - 1]))[:2]
        if beside is not None and step > 1:
            passed.append(
                spread(tie(passed[-1] if passed else beside[None], first), count >> (step - 1))
            )
        first, second = lax.ppermute(first, "band", onward), lax.ppermute(second, "band", back)
        if marks is not None:
            marks.append((first, second))
        blocks = put(blocks, first, place - step)
        blocks = put(blocks, second, place + step)
    cut = -(-half // 256) * 128
    first, second = lax.optimization_barrier(
        (first[:, :cut], second[:, cut:], *gates[middle - 1], *(passed or ())[-2:-1])
    )[:2]
    while beside is not None and len(passed) < count.bit_length() - 1:
        passed.append(
            spread(tie(passed[-1] if passed else beside[None], first), count >> (len(passed) + 1))
        )
    first, second = lax.ppermute(first, "band", onward), lax.ppermute(second, "band", back)
    blocks = put(blocks, first, place - middle)
    return put(blocks, second, place - middle, cut)


def spread(value, step):
    bit = (lax.axis_index("band") // step) % 2
    value = both(value, swap_bands(value, step), bit, 1)
    return value.reshape(-1, *value.shape[2:])


def gather_doubling(shard, *gates):
    value, values = shard[None], []
    step = lax.axis_size("band") // 2
    gates = [*gates, *[()] * lax.axis_size("band")]
    while step:
        value = spread(tie(value, *gates[len(values)]), step)
        values.append(value)
        step //= 2
    return values


def halve(parts, step):
    parts = parts.reshape(-1, 2, *parts.shape[1:])
    bit = (lax.axis_index("band") // step) % 2
    sent = lax.dynamic_index_in_dim(parts, 1 - bit, 1, False)
    kept = lax.dynamic_index_in_dim(parts, bit, 1, False)
    total = kept.astype(jnp.float32) + swap_bands(sent, step).astype(jnp.float32)
    return total.astype(jnp.bfloat16)


def halve_pairs(parts):
    parts = parts.reshape(parts.shape[0], 2, -1, parts.shape[2])
    bit = lax.axis_index("pair")
    sent = lax.dynamic_index_in_dim(parts, 1 - bit, 1, False)
    kept = lax.dynamic_index_in_dim(parts, bit, 1, False)
    total = kept.astype(jnp.float32) + swap_pairs(sent).astype(jnp.float32)
    return total.astype(jnp.bfloat16)


def gather_bands(shard):
    return lax.all_gather(shard, SEQ, axis=0, tiled=True)


def in_order(own, other):
    first = lax.axis_index("core") == 0
    return jnp.concatenate([jnp.where(first, own, other), jnp.where(first, other, own)], -1)


def both_cores(own, other):
    return (own + other_core(other.astype(jnp.bfloat16)).astype(jnp.float32)).astype(jnp.bfloat16)


def sum_bands(total):
    if lax.axis_size("ring") > 1:
        return lax.psum_scatter(total, SEQ, scatter_dimension=0, tiled=True)
    bands = lax.axis_size("band")
    parts = total.reshape(bands, total.shape[0] // bands, total.shape[1])
    return jnp.sum(exchange(parts).astype(jnp.float32), 0).astype(jnp.bfloat16)


def sum_pairs(total):
    pairs = lax.axis_size("pair")
    if pairs == 1:
        return total
    if pairs == 2:
        return (total.astype(jnp.float32) + swap_pairs(total).astype(jnp.float32)).astype(total.dtype)
    return lax.psum(total, "pair")


def ordered(total):
    return in_order(total, other_core(total)).astype(jnp.float32)


def sum_everywhere(value):
    if not doubling():
        return lax.psum(value, SEQ)
    step = 1
    while step < lax.axis_size("band"):
        value = value + swap_bands(value, step)
        step *= 2
    return value


def tie(value, *others):
    return lax.optimization_barrier((value, *others))[0] if others else value


def as_line(scalars, width):
    line = jnp.concatenate([scalar.reshape(-1) for scalar in scalars])
    return jnp.pad(line, (0, width - line.size))[None]


def split_rows(rows, counts):
    results, place = [], 0
    for count in counts:
        results.append(rows[place : place + count])
        place += count
    return results


def factor_parts(gradient, rows_old, decay_rate):
    square = gradient * gradient + square_floor
    rows_new = decay_rate * rows_old + (1.0 - decay_rate) * jnp.mean(square, -1)
    ratio_part = jnp.sum(gradient * gradient / rows_new[..., None], -2)
    return rows_new, jnp.sum(square, -2), ratio_part, jnp.sum(rows_new, -1)


def lane(line, place):
    lanes = lax.broadcasted_iota(jnp.int32, line.shape, 1)
    return jnp.sum(jnp.where(lanes == place, line, 0.0), 1, keepdims=True)


def lanes_down(line, place, count):
    lanes = lax.broadcasted_iota(jnp.int32, (count, line.shape[1]), 1)
    rows = lax.broadcasted_iota(jnp.int32, (count, line.shape[1]), 0)
    return jnp.sum(jnp.where(lanes == rows + place, line, 0.0), 1, keepdims=True)


AT_ATTENTION, AT_FORWARD, AT_SQUARES, AT_VECTOR_SQUARES, AT_VECTOR_SIZES = 0, 4, 6, 128, 256
ROW_ATTENTION, ROW_FORWARD, ROW_LINE, ROW_SMALL = 0, 8, 24, 25


def patch_kernel(core_ref, own_ref, other_ref, rows_ref, grad_ref, rows_new_ref, pack_ref):
    decay_rate = 1.0 - STEP ** (-0.8)
    own, other = own_ref[...].astype(jnp.float32), other_ref[...].astype(jnp.float32)
    first = core_ref[0] == 0
    gradient = jnp.concatenate(
        [jnp.where(first, own, other), jnp.where(first, other, own)], 1
    )
    grad_ref[...] = gradient
    plain = gradient * gradient
    square = plain + square_floor
    rows_new = decay_rate * rows_ref[...] + (1.0 - decay_rate) * jnp.mean(square, 1, keepdims=True)
    rows_new_ref[...] = rows_new
    width = gradient.shape[1]
    pack = jnp.concatenate(
        [
            jnp.sum(square, 0, keepdims=True),
            jnp.sum(plain / rows_new, 0, keepdims=True),
            jnp.broadcast_to(jnp.sum(rows_new, 0, keepdims=True), (1, width)),
            jnp.zeros((5, width), jnp.float32),
        ],
        0,
    )
    for copy in range(pack_ref.shape[0]):
        pack_ref[copy] = pack


def patch_statistics(own, other, rows_old, copies):
    rows, half = own.shape
    width = 2 * half
    space = [pl.BlockSpec(memory_space=pltpu.VMEM)]
    return pl.pallas_call(
        patch_kernel,
        in_specs=[pl.BlockSpec(memory_space=pltpu.SMEM)] + space * 3,
        out_specs=space * 3,
        out_shape=[
            jax.ShapeDtypeStruct((rows, width), jnp.float32),
            jax.ShapeDtypeStruct((rows, 1), jnp.float32),
            jax.ShapeDtypeStruct((copies, 8, width), jnp.float32),
        ],
        compiler_params=pltpu.CompilerParams(vmem_limit_bytes=vmem_limit),
        name="patch_statistics",
    )(lax.axis_index("core").reshape(1), own, other, rows_old.reshape(rows, 1))


def finish_matrix(
    grad, master, rows_new, olds, sums, ratios, rows_total, weight_total, band_count, store
):
    decay_rate = 1.0 - STEP ** (-0.8)
    width = sums[0].shape[1]
    row_count = grad.shape[0] * band_count
    element_count = row_count * width * len(olds)
    columns_new = [
        decay_rate * old + (1.0 - decay_rate) / row_count * part for old, part in zip(olds, sums)
    ]
    mean_rows = rows_total / row_count
    spread_sum = sum(
        jnp.sum(ratio / column, 1, keepdims=True) for ratio, column in zip(ratios, columns_new)
    )
    mean_square = mean_rows * spread_sum / element_count
    shrink = jnp.maximum(1.0, jnp.sqrt(mean_square) / clip_limit)
    rate_value = relative_rate * jnp.sqrt(weight_total / element_count)
    row_scale = lax.rsqrt(rows_new) * (jnp.sqrt(mean_rows) * rate_value / shrink)
    for piece, column in enumerate(columns_new):
        part = slice(piece * width, (piece + 1) * width)
        store(part, column, master[:, part] - grad[:, part] * row_scale * lax.rsqrt(column))


def patch_finish_kernel(
    pack_ref, square_ref, grad, master, rows_new, columns, master_new, columns_new, *, band_count
):
    pack = jnp.sum(pack_ref[...], 0)

    def store(part, column, value):
        master_new[:, part] = value
        columns_new[:, part] = column

    finish_matrix(
        grad,
        master,
        rows_new[...],
        [columns[...]],
        [pack[0:1]],
        [pack[1:2]],
        pack[2:3, :1],
        square_ref[...],
        band_count,
        store,
    )


def rest_finish_kernel(
    pack_ref,
    attention_grad, attention_master, attention_rows, attention_columns,
    forward_grad, forward_master, forward_rows, forward_columns,
    vectors, vector_update, lead_average,
    attention_new, attention_columns_new, forward_new, forward_columns_new,
    vectors_new, lead_new, patch_square,
    *, band_count,
):
    pack = jnp.sum(pack_ref[...], 0)
    width = pack.shape[1]
    line = pack[ROW_LINE : ROW_LINE + 1, :512]
    patch_square[...] = lane(line, AT_SQUARES + 6)
    for k in range(4):
        def attention_store(part, column, value):
            attention_new[k, :, part] = value
            attention_columns_new[k : k + 1, part] = column

        row = ROW_ATTENTION + k
        finish_matrix(
            attention_grad.at[k],
            attention_master.at[k],
            attention_rows[k],
            [attention_columns[k : k + 1, :]],
            [pack[row : row + 1]],
            [pack[row + 4 : row + 5]],
            lane(line, AT_ATTENTION + k),
            lane(line, AT_SQUARES + 2 + k),
            band_count,
            attention_store,
        )
    pieces = forward_grad.shape[2] // width
    for k in range(2):
        def forward_store(part, column, value):
            forward_new[k, :, part] = value
            forward_columns_new[k : k + 1, part] = column

        rows = [ROW_FORWARD + 2 * piece + k for piece in range(pieces)]
        finish_matrix(
            forward_grad.at[k],
            forward_master.at[k],
            forward_rows[k],
            [forward_columns[k : k + 1, p * width : (p + 1) * width] for p in range(pieces)],
            [pack[row : row + 1] for row in rows],
            [pack[row + 2 * pieces : row + 2 * pieces + 1] for row in rows],
            lane(line, AT_FORWARD + k),
            lane(line, AT_SQUARES + k),
            band_count,
            forward_store,
        )
    count = vectors.shape[0]
    vector_squares = lanes_down(line, AT_VECTOR_SQUARES, count)
    vector_sizes = lanes_down(line, AT_VECTOR_SIZES, count)
    vector_shrink = jnp.maximum(1.0, jnp.sqrt(vector_squares / width) / clip_limit)
    vector_rate = relative_rate * jnp.sqrt(vector_sizes / width)
    vectors_new[...] = vectors[...] - vector_rate / vector_shrink * vector_update[...]
    sums = pack[ROW_SMALL : ROW_SMALL + 1, :128]
    counts = pack[ROW_SMALL : ROW_SMALL + 1, 128:256]
    average = lead_average[...]
    batch_mean = jnp.where(counts > 0, sums / jnp.maximum(counts, 1.0), average)
    new_average = average_decay * average + (1.0 - average_decay) * batch_mean
    lead_new[0:1] = new_average
    lead_new[1:2] = new_average / (1.0 - average_decay**STEP)


def in_vmem(kernel, name, arguments, shapes, **fixed):
    space = pl.BlockSpec(memory_space=pltpu.VMEM)
    return pl.pallas_call(
        functools.partial(kernel, **fixed),
        in_specs=[space] * len(arguments),
        out_specs=[space] * len(shapes),
        out_shape=[jax.ShapeDtypeStruct(shape, jnp.float32) for shape in shapes],
        compiler_params=pltpu.CompilerParams(vmem_limit_bytes=vmem_limit),
        name=name,
    )(*arguments)


def finish_patch(pack, square, gradient, master, rows_new, columns, band_count):
    columns = columns.reshape(1, -1)
    arguments = (pack, square, gradient, master, rows_new, columns)
    return in_vmem(
        patch_finish_kernel,
        "patch_finish",
        arguments,
        (master.shape, columns.shape),
        band_count=band_count,
    )


def finish_rest(pack, attention, forward, vectors, vector_update, lead_average, band_count):
    def columns(parts):
        return (parts[0], parts[1], parts[2].reshape(*parts[2].shape, 1), parts[3])

    lead_line = jnp.pad(lead_average.reshape(1, -1), ((0, 0), (0, 128 - lead_average.size)))
    arguments = (pack, *columns(attention), *columns(forward), vectors, vector_update, lead_line)
    shapes = [array.shape for parts in (attention, forward) for array in (parts[1], parts[3])]
    shapes += [vectors.shape, (2, 128), (1, 1)]
    return in_vmem(rest_finish_kernel, "rest_finish", arguments, shapes, band_count=band_count)


def local(
    patches,
    channel_mask,
    lead_index,
    patch_weight,
    attention_weight,
    forward_weight,
    vectors,
    patch_rows,
    patch_columns,
    attention_rows,
    attention_columns,
    forward_rows,
    forward_columns,
    vector_second,
    lead_average,
    output_cotangent,
    gate_cotangent,
):
    low = jnp.bfloat16
    frames, frame_rows, patch_width = patches.shape
    channels = channel_mask.shape[1]
    bands, rings = lax.axis_size("band"), lax.axis_size("ring")
    band_count = bands * rings
    width = patch_weight.shape[1]
    half = width // 2
    lead_count = vectors.shape[0] - 5
    share = attention_weight.shape[1]
    vector_columns = vectors.shape[1]
    heads = frames * H // bands
    groups = H // heads
    decay_rate = 1.0 - STEP ** (-0.8)
    pair = lax.axis_index("pair")

    def weight_square(master):
        return jnp.sum(master * master, (-2, -1))

    squares = jnp.concatenate(
        [
            weight_square(forward_weight),
            weight_square(attention_weight),
            weight_square(patch_weight).reshape(1),
            jnp.sum(vectors * vectors, -1),
        ]
    )
    kinds = attention_weight[:3] * jnp.array([HD ** (-0.5), 1.0, 1.0], jnp.float32)[:, None, None]
    kinds = kinds.astype(low).reshape(3, share, groups, heads, HD)
    kinds = [
        jnp.transpose(kinds[:, :, :, j], (1, 2, 0, 3)).reshape(share, width) for j in range(heads)
    ]
    vector_part = jnp.pad(vectors.T.astype(low), ((0, 0), (0, 256 - vectors.shape[0])))
    first_shard = jnp.concatenate(
        [core_half(piece, 1, True) for piece in (kinds[0], vector_part)], 1
    )
    later_shard = jnp.concatenate(
        [core_half(piece, 1, True) for piece in (*kinds[1:], attention_weight[3].astype(low))], 1
    )
    patch_own = core_half(patch_weight, 1, True).astype(low)
    if doubling():
        marks, passed = [], []
        patch_full = ring_gather(
            patch_own, [], [first_shard], both_cores=True, marks=marks, passed=passed,
            beside=first_shard,
        )
        patch_full = patch_full.reshape(patch_width, width)
        first_own = passed[-1].reshape(width, first_shard.shape[1])
        later_steps = gather_doubling(pair_half(later_shard), [patch_full])
    else:
        first_own = gather_bands(first_shard)
        patch_own = gather_bands(patch_own)
        patch_full = in_order(patch_own, other_core(patch_own))
        later_steps = []
    first_other = other_core(first_own)
    projections = [in_order(first_own[:, :half], first_other[:, :half])]
    vector_full = in_order(first_own[:, half:], first_other[:, half:])[:, : vectors.shape[0]].T
    vector_full = vector_full.astype(jnp.float32)
    patch_full, squares = lax.optimization_barrier((patch_full, squares))
    hidden_half = forward_weight.shape[2] // 2
    forward_shard = core_half(forward_weight, 2, True).astype(low)
    forward_shard = jnp.concatenate([forward_shard[0], forward_shard[1]], 1)
    mask_values = channel_mask.astype(low)
    masked = (
        patches.reshape(frames, frame_rows, channels, patch_width // channels)
        * mask_values[:, None, :, None]
    ).reshape(frames, frame_rows, patch_width)
    embedded = jnp.einsum("fsp,pd->fsd", masked, patch_full, preferred_element_type=jnp.float32)
    lead_hot = (lead_index[:, None] == jnp.arange(lead_count, dtype=jnp.int32)[None, :]).astype(
        jnp.float32
    )
    lead_rows = jnp.dot(lead_hot, vector_full[5:], precision=highest)
    residual_zero = embedded + lead_rows[:, None, :]
    gain_one, gain_two, head_rows = vector_full[0], vector_full[1], vector_full[2:5]
    normed_one, standard_one, inverse_one = norm_forward(residual_zero, gain_one)
    normed_one = normed_one.astype(low)

    if doubling():
        normed_one = tie(normed_one, later_steps[-2])
    def project(j, *before):
        projected = jnp.einsum(
            "dm,fsd->fms", projections[j], tie(normed_one, *before), preferred_element_type=jnp.float32
        ).astype(low)
        return projected.reshape(bands, 3, HD, frame_rows)

    received, triples, attended_here, log_totals = [], [], [], []

    def run_head(number, before):
        triple, here, totals = run_forward(received[number], before)
        triples.append(triple)
        attended_here.append(here)
        log_totals.append(totals)

    first_sent = project(0)
    received.append(exchange(first_sent))
    if doubling():
        later_own = tie(later_steps[-1], first_sent).reshape(-1, later_shard.shape[1])
        later_own = join_pairs(later_own, bands)
    else:
        later_own = gather_bands(later_shard)
    later_other = other_core(later_own)
    projections += [
        in_order(later_own[:, j * half : (j + 1) * half], later_other[:, j * half : (j + 1) * half])
        for j in range(heads - 1)
    ]
    place = (heads - 1) * half
    output_weight = in_order(later_own[:, place:], later_other[:, place:])
    second_sent = [project(1)] if heads > 1 else []
    marks = []
    if doubling():
        forward_own = ring_gather(pair_half(forward_shard), second_sent, marks=marks)
        forward_own = forward_own.reshape(-1, 2 * hidden_half)
    else:
        forward_own = gather_bands(forward_shard)
    forward_parts = forward_own[:, :hidden_half], forward_own[:, hidden_half:]
    swapped = ()
    if doubling():
        forward_parts = tuple(part.reshape(bands, -1, hidden_half) for part in forward_parts)
        swapped = tuple(swap_pairs(part) for part in forward_parts)

    def forward_half(number):
        part = forward_parts[number]
        if doubling():
            part, received, _ = lax.optimization_barrier(
                (part, swapped[number], attended_here[-1])
            )
            part = both(part, received, pair, 1).reshape(width, hidden_half)
        return part, other_core(part)

    for j in range(1, heads):
        sent = second_sent[0] if j == 1 else project(j)
        sent = tie(sent, received[j - 1], *attended_here[j - 2 : j - 1])
        received.append(exchange(sent))
        before = [sent] if j == 1 else [attended_here[-1]]
        before += [part for step in marks[1:2] for part in step if j == 2]
        run_head(j - 1, before)
    before = [forward_own, *attended_here[-1:]]
    chunks = received[-1].shape[0]
    if rings == 1 and heads > 1 and chunks % 4 == 0:
        triple, here, totals = run_forward(received[-1], before, 0, chunks * 3 // 4)
        attended = exchange(tie(jnp.concatenate(attended_here, 1), received[-1]))
        _, here_end, totals_end = run_forward(
            received[-1], [here, attended, *swapped[:1]], chunks * 3 // 4, chunks // 4
        )
        triples.append(triple)
        attended_here.append(jnp.concatenate([here, here_end], 0))
        log_totals.append(jnp.concatenate([totals, totals_end], 1))
        attended = jnp.concatenate([attended, exchange(attended_here[-1])], 1)
    else:
        run_head(heads - 1, before)
        attended = jnp.concatenate([split_chunks(here, bands) for here in attended_here], 1)
        attended = exchange(attended)
    attended = attended.reshape(frames, width, frame_rows)
    up_halves, down_halves = forward_half(0), forward_half(1)

    residual_one = residual_zero + jnp.einsum(
        "fns,nd->fsd", attended, output_weight, preferred_element_type=jnp.float32
    )
    normed_two, standard_two, inverse_two = norm_forward(residual_one, gain_two)
    normed_two = normed_two.astype(low)

    hidden, slopes = [], []
    residual_two = residual_one
    for up, down in zip(up_halves, down_halves):
        upward = jnp.einsum("fsd,dh->fsh", normed_two, up, preferred_element_type=jnp.float32)
        activated, slope = gelu_pair(upward)
        hidden.append(activated.astype(low))
        slopes.append(slope)
        residual_two = residual_two + jnp.einsum(
            "fsh,dh->fsd", hidden[-1], down, preferred_element_type=jnp.float32
        )
    logits = jnp.einsum("fsd,ed->fes", residual_two, head_rows, precision=highest)
    expert_gates = jax.nn.softmax(logits, axis=1)
    logit_grad = expert_gates * (
        gate_cotangent - jnp.sum(expert_gates * gate_cotangent, 1, keepdims=True)
    )
    adjoint_two = output_cotangent.astype(jnp.float32) + jnp.einsum(
        "fes,ed->fsd", logit_grad, head_rows, precision=highest
    )
    adjoint_two_low = adjoint_two.astype(low)
    upward_grad = []
    normed_two_grad = 0.0
    for up, down, slope in zip(up_halves, down_halves, slopes):
        hidden_grad = jnp.einsum(
            "fsd,dh->fsh", adjoint_two_low, down, preferred_element_type=jnp.float32
        )
        upward_grad.append((hidden_grad * slope).astype(low))
        normed_two_grad = normed_two_grad + jnp.einsum(
            "fsh,dh->fsd", upward_grad[-1], up, preferred_element_type=jnp.float32
        )
    through_two, gain_two_grad = norm_backward(normed_two_grad, standard_two, inverse_two, gain_two)
    adjoint_one = adjoint_two + through_two
    adjoint_one_low = adjoint_one.astype(low)
    attended_grad = jnp.einsum(
        "fsd,nd->fns", adjoint_one_low, output_weight, preferred_element_type=jnp.float32
    ).astype(low)
    attended_grad = attended_grad.reshape(bands, 1, heads, HD, frame_rows)
    first_outgrad = attended_grad[:, :, 0]
    first_grad = exchange(first_outgrad)
    outgrads = [(join_chunks(first_grad), 0)]
    if heads > 1:
        later_sent = attended_grad[:, 0, 1:]

    early_left = lax.optimization_barrier((normed_two, adjoint_two_low, first_outgrad))[:2]

    def early_product(left, right):
        return jnp.einsum("fsd,fsh->dh", left, right, preferred_element_type=jnp.float32)

    early = jnp.concatenate(
        [
            both_cores(early_product(left, right[0]), early_product(left, right[1]))
            for left, right in zip(early_left, (upward_grad, hidden))
        ],
        1,
    )
    outgrads[0] = (tie(outgrads[0][0], early), 0)
    if heads > 1:
        later = join_chunks(exchange(tie(later_sent, first_grad, early)))
        outgrads += [(later, j) for j in range(heads - 1)]
    early_stages = []
    if doubling():
        stage = halve_pairs(early.reshape(bands, -1, early.shape[1]))
        early_stages.append(stage)
        step = 1
        while step < bands and len(early_stages) < heads:
            if step == 1:
                stage = tie(stage, first_grad)
            stage = halve(stage, step)
            early_stages.append(stage)
            step *= 2

    head_grads = []
    for j in range(heads):
        query, key, value = triples[j]
        outgrad = outgrads[j]
        if j > 0:
            outgrad = (
                tie(outgrad[0], grads, *early_stages[j - 1 : j], *head_grads[j - 2 : j - 1]),
                outgrad[1],
            )
        grads = attention_backward(
            query, outgrad, attended_here[j], log_totals[j], key, value, rings == 1
        )
        if rings == 1:
            parts = grads[0]
        else:
            parts = lax.psum_scatter(grads[1], "ring", scatter_dimension=0, tiled=True)
            parts = jnp.concatenate([grads[0], parts.astype(low)], 1)
        parts = exchange(tie(split_chunks(parts, bands), *head_grads[j - 1 : j]))
        head_grads.append(parts.reshape(frames, width, frame_rows))
    kernel_end = (*grads, *early_stages[heads - 1 : heads], *head_grads[heads - 2 : heads - 1])
    head_grads = [tie(part, *kernel_end) for part in head_grads[:-1]] + head_grads[-1:]

    normed_one_grad = 0.0
    for j in range(heads):
        normed_one_grad = normed_one_grad + jnp.einsum(
            "fms,dm->fsd", head_grads[j], projections[j], preferred_element_type=jnp.float32
        )
    through_one, gain_one_grad = norm_backward(normed_one_grad, standard_one, inverse_one, gain_one)
    adjoint_zero = adjoint_one + through_one
    adjoint_zero_low = adjoint_zero.astype(low)

    def projection_product(j, own_half):
        if j == heads:
            return jnp.einsum(
                "fns,fsd->nd",
                attended,
                core_half(tie(adjoint_one_low, *kernel_end), 2, own_half),
                preferred_element_type=jnp.float32,
            )
        return jnp.einsum(
            "fsd,fms->dm",
            normed_one,
            core_half(head_grads[j], 1, own_half),
            preferred_element_type=jnp.float32,
        )

    def projection_part(numbers):
        return both_cores(
            jnp.concatenate([projection_product(j, True) for j in numbers], 1),
            jnp.concatenate([projection_product(j, False) for j in numbers], 1),
        )

    def projection_start(total):
        if doubling():
            return halve_pairs(total.reshape(bands, -1, total.shape[1]))
        return total

    def projection_exchange(total):
        return exchange(total) if doubling() else sum_bands(total)

    def projection_sums(total):
        if doubling():
            return join_pairs(jnp.sum(total.astype(jnp.float32), 0).astype(low), 1)
        return sum_pairs(total)

    earlier = projection_part([*range(heads - 1), heads])

    def patch_product(columns):
        return jnp.einsum("fsp,fsd->pd", masked, columns, preferred_element_type=jnp.float32)

    own_adjoint = core_half(adjoint_zero_low, 2, True)
    other_adjoint = core_half(adjoint_zero_low, 2, False)
    cut = half * 2 // 3
    pieces = [
        both_cores(
            patch_product(own_adjoint[:, :, piece]), patch_product(other_adjoint[:, :, piece])
        )
        for piece in (slice(0, cut), slice(cut, half))
    ]
    sent = tuple(pieces)
    first_piece = sum_bands(pieces[0])

    pixel_term = jnp.einsum(
        "fsd,pd->fsp", tie(adjoint_zero_low, *sent), patch_full, preferred_element_type=jnp.float32
    )
    pixel_gradient = (
        (
            pixel_term.reshape(frames, frame_rows, channels, -1)
            * mask_values.astype(jnp.float32)[:, None, :, None]
        )
        .reshape(frames, frame_rows, patch_width)
        .astype(low)
    )

    head_grads[-1] = tie(head_grads[-1], *sent)
    lead_sums = jnp.dot(lead_hot.T, jnp.sum(tie(expert_gates, *sent), 2), precision=highest)
    lead_counts = jnp.sum(lead_hot, 0) * frame_rows
    small = jnp.concatenate(
        [
            jnp.pad(value, (0, 128 - value.size))
            for value in (lead_sums.reshape(-1), jnp.repeat(lead_counts, 3))
        ]
    )
    small = jnp.pad(small, (0, width - small.size))[None]
    if lax.axis_size("pair") == 2:
        small = small + swap_pairs(small)
    elif lax.axis_size("pair") > 1:
        small = lax.psum(small, "pair")
    small = small + other_core(small)
    lead_term = jnp.dot(lead_hot.T, jnp.sum(tie(adjoint_zero, *sent), 1), precision=highest)
    head_gradient = jnp.einsum(
        "fes,fsd->ed", tie(logit_grad, *sent), residual_two, precision=highest
    )
    vector_term = jnp.concatenate(
        [gain_one_grad[None], gain_two_grad[None], head_gradient, lead_term], 0
    )
    vector_term = jnp.pad(vector_term.T, ((0, 0), (0, 128 - vectors.shape[0])))
    total = jnp.concatenate(
        [earlier, projection_part([heads - 1]), both_cores(vector_term, vector_term)], 1
    )
    total = projection_start(total)
    total = projection_exchange(tie(total, first_piece, pixel_gradient))
    second_piece = sum_bands(tie(pieces[1], total))
    total = projection_sums(total)
    place = (heads + 1) * half
    vector_gradient = total[:, place : place + vectors.shape[0]].T.astype(jnp.float32)
    total = total[:, :place]
    total_other = other_core(total)
    parts = [
        in_order(total[:, j * half : (j + 1) * half], total_other[:, j * half : (j + 1) * half])
        for j in range(heads + 1)
    ]
    output_gradient = parts.pop(heads - 1)
    projection_gradient = jnp.transpose(
        jnp.stack(parts).reshape(heads, share, groups, 3, HD), (3, 1, 2, 0, 4)
    ).reshape(3, share, width)
    kind_scales = jnp.array([HD ** (-0.5), 1.0, 1.0, 1.0], jnp.float32)[:, None, None]
    attention_gradient = with_layout_constraint(
        jnp.concatenate([projection_gradient, output_gradient[None]], 0).astype(jnp.float32)
        * kind_scales,
        Layout(major_to_minor=(0, 1, 2)),
    )

    if doubling():
        stage = tie(early_stages[-1], *sent)
        step = 1 << (len(early_stages) - 1)
        while step < bands:
            stage = halve(stage, step)
            step *= 2
        early = join_pairs(stage[0], 1)
    else:
        early = sum_pairs(sum_bands(tie(early, *sent)))
    early_other = other_core(early)
    forward_gradient = jnp.stack(
        [
            in_order(early[:, :hidden_half], early_other[:, :hidden_half]),
            in_order(early[:, hidden_half:], early_other[:, hidden_half:]),
        ]
    ).astype(jnp.float32)
    units = forward_weight.shape[2]
    forward_rows_new, forward_sums, forward_ratios, forward_total = factor_parts(
        forward_gradient, forward_rows, decay_rate
    )

    vector_second_new = decay_rate * vector_second + (1.0 - decay_rate) * (
        vector_gradient * vector_gradient + square_floor
    )
    vector_update = vector_gradient * lax.rsqrt(vector_second_new)
    vector_squares = jnp.sum(vector_update * vector_update, -1)

    attention_rows_new, attention_sums, attention_ratios, attention_total = factor_parts(
        attention_gradient, attention_rows, decay_rate
    )
    pieces = units // width
    line = jnp.concatenate(
        [
            jnp.pad(value, (0, 128 - value.size))
            for value in (
                jnp.concatenate([attention_total, forward_total, squares[:7]]),
                vector_squares,
                squares[7:],
            )
        ]
    )
    rest = jnp.concatenate(
        [attention_sums, attention_ratios]
        + [
            part[:, piece * width : (piece + 1) * width]
            for part in (forward_sums, forward_ratios)
            for piece in range(pieces)
        ]
        + [jnp.pad(line, (0, width - line.size))[None], small],
        0,
    )
    def over_bands(copies):
        return exchange(copies) if rings == 1 else lax.psum(copies, SEQ)

    copies = bands if rings == 1 else 1
    rest = tie(jnp.broadcast_to(rest, (copies, *rest.shape)), second_piece)
    rest_sums = over_bands(rest)
    patch_own_sum = sum_pairs(tie(jnp.concatenate([first_piece, second_piece], 1), rest))
    patch_gradient, patch_rows_new, pack = patch_statistics(
        patch_own_sum, other_core(patch_own_sum), patch_rows, copies
    )
    pack = over_bands(tie(pack, rest_sums))
    (
        attention_weight_new,
        attention_columns_new,
        forward_weight_new,
        forward_columns_new,
        vectors_new,
        lead_new,
        patch_square,
    ) = finish_rest(
        rest_sums,
        (attention_gradient, attention_weight, attention_rows_new, attention_columns),
        (forward_gradient, forward_weight, forward_rows_new, forward_columns),
        vectors,
        vector_update,
        lead_average,
        band_count,
    )
    patch_rows_line = patch_rows_new[:, 0]
    pack, patch_rows_line = lax.optimization_barrier((pack, patch_rows_line))
    patch_weight_new, patch_columns_new = finish_patch(
        pack, patch_square, patch_gradient, patch_weight, patch_rows_new, patch_columns, band_count
    )
    lead_stats = lead_new[:, : lead_average.size].reshape(2, *lead_average.shape)
    return (
        residual_two.astype(low),
        expert_gates,
        pixel_gradient,
        patch_gradient,
        attention_gradient,
        forward_gradient,
        vector_gradient,
        patch_rows_line,
        patch_columns_new[0],
        attention_rows_new,
        attention_columns_new,
        forward_rows_new,
        forward_columns_new,
        vector_second_new,
        patch_weight_new,
        attention_weight_new,
        forward_weight_new,
        vectors_new,
        lead_stats,
    )


def solution(mesh):
    seq, dp = mesh.shape["seq"], mesh.shape["dp"]
    cores = 2 if dp % 2 == 0 else 1
    dp_axes = ("pair", "core")
    row_spec = P(None, SEQ, None)

    def step(*arguments):
        bands = math.gcd(arguments[0].shape[0] // dp * H, seq)
        grid_mesh = Mesh(
            mesh.devices.reshape(seq // bands, bands, dp // cores, cores),
            ("ring", "band", "pair", "core"),
        )
        return jax.shard_map(
            local,
            mesh=grid_mesh,
            in_specs=(
                P(dp_axes, SEQ, None),
                P(dp_axes, None),
                P(dp_axes),
                P(SEQ, None),
                row_spec,
                row_spec,
                P(None, SEQ),
                P(SEQ),
                P(),
                P(None, SEQ),
                P(),
                P(None, SEQ),
                P(),
                P(None, SEQ),
                P(),
                P(dp_axes, SEQ, None),
                P(dp_axes, None, SEQ),
            ),
            out_specs=(
                P(dp_axes, SEQ, None),
                P(dp_axes, None, SEQ),
                P(dp_axes, SEQ, None),
                P(SEQ, None),
                row_spec,
                row_spec,
                P(None, SEQ),
                P(SEQ),
                P(),
                P(None, SEQ),
                P(),
                P(None, SEQ),
                P(),
                P(None, SEQ),
                P(SEQ, None),
                row_spec,
                row_spec,
                P(None, SEQ),
                P(),
            ),
            check_vma=False,
        )(*arguments)

    return step
```

time: 3900 us -> 840 us (0.22)
  waiting for transfers between devices: 1790 us -> 194 us
  blocking collectives: 574 us -> 0 us
  matrix products: 647 us -> 148 us
  local copies, waits for them, and re-layouts: 474 us -> 88.9 us
  other arithmetic: 349 us -> 59.1 us
  Pallas kernels: 0 us -> 225 us
  starting transfers between devices: 0.58 us -> 115 us
  loops' own time: 39.8 us -> 0 us
    reduce_scatter x3 -> x0, waiting for transfers between devices: 1000 us -> none  [the longest x1 768 us: local(): lax.psum_scatter(kv_terms, 'seq', scatter_dimension=3, tiled=True)]
    all_gather x4 -> x0, waiting for transfers between devices: 612 us -> none  [the longest x1 472 us: local(): full_kv = lax.all_gather(projected[1:], 'seq', axis=2, tiled=True)]
    dot_general x102 -> x37, matrix products: 631 us -> 132 us  [the longest x4 17.5 us: early_product(): jnp.einsum('fsd,fsh->dh', left, right, preferred_element_type=jnp.float32)]
    unnamed x1 -> x0, blocking collectives: 441 us -> none
    slice x25 -> x16, local copies, waits for them, and re-layouts: 334 us -> 4.75 us  [the longest x1 2.79 us: local(): forward_parts = (forward_own[:, :hidden_half], forward_own[:, hidden_half:])]
    pallas_call x0 -> x10, Pallas kernels: none -> 225 us  [the longest x3 136 us: attention_backward(): pl.pallas_call(functools.partial(backward_kernel, merged=merged), grid=(h...]
    psum x2 -> x0, waiting for transfers between devices: 170 us -> none  [the longest x1 106 us: local(): lax.psum((vector_term, lead_sums, lead_counts), ('seq', 'dp'))]
    convert_element_type x18 -> x15, other arithmetic: 172 us -> 17.1 us  [the longest x2 3.9 us: halve_pairs(): return total.astype(jnp.bfloat16)]
  transfers between devices with their start and end apart: 9 -> 73, of which waited for: 7 -> 26; matrix products, arithmetic and copies ran while one was open for 16% -> 31% of each run, Pallas kernels for 0% -> 26%
where the time goes in v1:
time: 840 us; the launch traced here: 832 us
  Pallas kernels  225 us (27%)
  waiting for transfers between devices  194 us (23%)
  matrix products  148 us (18%)
  starting transfers between devices  115 us (14%)
  local copies, waits for them, and re-layouts  88.9 us (11%)
  other arithmetic  59.1 us (7%)
    pallas_call x3, Pallas kernels, attention_backward(): pl.pallas_call(functools.partial(backward_kernel, merged=merged), grid=(h...  136 us
    all_to_all x15, waiting for transfers between devices, exchange(): return lax.all_to_all(parts, 'band', 0, 0, tiled=True)  87.7 us
    pallas_call x4, Pallas kernels, attention_forward(): pl.pallas_call(forward_kernel, grid=(heads, q_chunks), in_specs=[token_bl...  75.2 us
    all_to_all x15, starting transfers between devices, exchange(): return lax.all_to_all(parts, 'band', 0, 0, tiled=True)  72.8 us
    ppermute x9, waiting for transfers between devices, swap_pairs(): return lax.ppermute(value, 'pair', [(0, 1), (1, 0)])  59.4 us
    ppermute x9, waiting for transfers between devices, swap_bands(): lax.ppermute(value, 'band', [(i, i ^ step) for i in range(lax.axis_size('...  28.9 us
    dynamic_update_slice x17, local copies, waits for them, and re-layouts, put(): return lax.dynamic_update_slice(blocks, part[None], (source, 0, column))  19.9 us
    dot_general x4, matrix products, early_product(): jnp.einsum('fsd,fsh->dh', left, right, preferred_element_type=jnp.float32)  17.5 us
  transfers between devices with their start and end apart: 73, of which 26 were waited for; matrix products, arithmetic and copies ran while one was open for 31% of the time, Pallas kernels for 26%

profile of v1, /device:TPU:0, one launch (start us, length us, event | category | flops | bytes accessed | tf_op | source)
XLA Modules:
  0.0 832.4 jit_solution(9081449428606856805)
XLA Ops:
  30.1 6.9 collective-permute-done.13
  44.1 7.5 collective-permute-done.18
  70.0 6.8 collective-permute-done.21
  78.5 5.5 collective-permute-done.22
  85.6 12.6 %add_reduce_fusion = (f32[2,512]{1,0:T(2,128)S(1)}, f32[2,512,768]{2,1,0:T(8,128)S(1)}) fusion(f32[2,768]{1,0:T(2,128)S(1)} %fusion.81, bf16[4416,768]{1,0:T(8,128)(2,1)} %bitcast.27, bf16[2,512,4416]{1,2,0:T(8,128)(2,1)} %param.19, bf16[2,4416]{1,0:T(2,128)(2,1)S(1)} %mul.374), kind=kOutput, calls=%fused_computation.69 | convolution fusion | flops 6951861248 | bytes 19000576 | tf_op jit(solution)/shard_map/fsp,pd->fsd/dot_general | solution.py:789
  114.7 14.5 %collective-permute-done.24 = bf16[8,48,1152]{2,1,0:T(8,128)(2,1)} collective-permute-done((bf16[8,48,1152]{2,1,0:T(8,128)(2,1)}, bf16[8,48,1152]{2,1,0:T(8,128)(2,1)}, u32[]{:S(2)}, u32[]{:S(2)}) %collective-permute-start.24) | collective-permute-done | bytes 884768 | tf_op jit(solution)/shard_map/ppermute | solution.py:311
  150.5 4.7 all-to-all-start.1
  155.3 24.4 %attention_forward.4 = (bf16[8,1,64,512]{3,2,1,0:T(8,128)(2,1)}, f32[1,8,1,512]{3,2,1,0:T(1,128)}) custom-call(bf16[8,3,64,512]{3,2,1,0:T(8,128)(2,1)} %all-to-all-done.q_ref.k_ref.v_ref, bf16[8,3,64,512]{3,2,1,0:T(8,128)(2,1)} %all-to-all-done.q_ref.k_ref.v_ref, bf16[8,3,64,512]{3,2,1,0:T(8,128)(2,1)} %all-to-all-done.q_ref.k_ref.v_ref), custom_call_target="tpu_custom_call" | custom-call | flops 17179869184 | bytes 4194304 | tf_op jit(solution)/shard_map/attention_forward/pallas_call | solution.py:206
  192.8 5.0 collective-permute-done.29
  201.3 4.9 collective-permute-done.30
  219.6 24.3 %attention_forward.5 = (bf16[8,1,64,512]{3,2,1,0:T(8,128)(2,1)}, f32[1,8,1,512]{3,2,1,0:T(1,128)}) custom-call(bf16[8,3,64,512]{3,2,1,0:T(8,128)(2,1)} %all-to-all-done.1.q_ref.k_ref.v_ref, bf16[8,3,64,512]{3,2,1,0:T(8,128)(2,1)} %all-to-all-done.1.q_ref.k_ref.v_ref, bf16[8,3,64,512]{3,2,1,0:T(8,128)(2,1)} %all-to-all-done.1.q_ref.k_ref.v_ref), custom_call_target="tpu_custom_call" | custom-call | flops 17179869184 | bytes 4194304 | tf_op jit(solution)/shard_map/attention_forward/pallas_call | solution.py:206
  246.1 4.3 all-to-all-done.2.q_ref.k_ref.v_ref
  259.5 18.7 %attention_forward.6 = (bf16[6,1,64,512]{3,2,1,0:T(8,128)(2,1)}, f32[1,6,1,512]{3,2,1,0:T(1,128)}) custom-call(bf16[8,3,64,512]{3,2,1,0:T(8,128)(2,1)} %all-to-all-done.2.q_ref.k_ref.v_ref, bf16[8,3,64,512]{3,2,1,0:T(8,128)(2,1)} %all-to-all-done.2.q_ref.k_ref.v_ref, bf16[8,3,64,512]{3,2,1,0:T(8,128)(2,1)} %all-to-all-done.2.q_ref.k_ref.v_ref), custom_call_target="tpu_custom_call" | custom-call | flops 12884901888 | bytes 3670016 | tf_op jit(solution)/shard_map/attention_forward/pallas_call | solution.py:206
  280.0 6.5 collective-permute-done.34
  286.5 7.7 attention_forward.7
  295.7 6.1 all-to-all-start.4
  301.9 7.8 collective-permute-done.35
  321.8 5.2 multiply_convert_fusion.2
  327.1 5.4 fusion.128
  332.5 5.2 multiply_convert_fusion.1
  337.7 5.5 fusion.126
  347.5 5.8 fusion.16
  357.5 5.2 fusion.10
  371.3 5.7 multiply_reduce_fusion
  381.8 6.2 all-to-all-start.5
  389.0 5.3 fusion.25
  403.2 6.1 all-to-all-start.7
  409.3 45.5 %attention_backward.3 = bf16[8,3,64,512]{3,2,1,0:T(8,128)(2,1)} custom-call(bf16[8,3,64,512]{3,2,1,0:T(8,128)(2,1)} %all-to-all-done.q_ref.k_ref.v_ref, bf16[8,1,64,512]{3,2,1,0:T(8,128)(2,1)} %all-to-all-done.5.g_ref, bf16[8,1,64,512]{3,2,1,0:T(8,128)(2,1)} %get-tuple-element.116.o_ref, f32[1,8,1,512]{3,2,1,0:T(1,128)} %get-tuple-element.140.lse_ref, ...), custom_call_target="tpu_custom_call" | custom-call | flops 42949672960 | bytes 8388608 | tf_op jit(solution)/shard_map/attention_backward/pallas_call | solution.py:251
  460.6 4.7 all-to-all-start.6
  465.4 45.4 %attention_backward.4 = bf16[8,3,64,512]{3,2,1,0:T(8,128)(2,1)} custom-call(bf16[8,3,64,512]{3,2,1,0:T(8,128)(2,1)} %all-to-all-done.1.q_ref.k_ref.v_ref, bf16[8,2,64,512]{3,2,1,0:T(8,128)(2,1)} %all-to-all-done.7.g_ref, bf16[8,1,64,512]{3,2,1,0:T(8,128)(2,1)} %get-tuple-element.122.o_ref, f32[1,8,1,512]{3,2,1,0:T(1,128)} %get-tuple-element.143.lse_ref, ...), custom_call_target="tpu_custom_call" | custom-call | flops 42949672960 | bytes 8388608 | tf_op jit(solution)/shard_map/attention_backward/pallas_call | solution.py:251
  510.8 6.0 all-to-all-start.8
  521.6 45.4 %attention_backward.5 = bf16[8,3,64,512]{3,2,1,0:T(8,128)(2,1)} custom-call(bf16[8,3,64,512]{3,2,1,0:T(8,128)(2,1)} %all-to-all-done.2.q_ref.k_ref.v_ref, bf16[8,2,64,512]{3,2,1,0:T(8,128)(2,1)} %all-to-all-done.7.g_ref, bf16[8,1,64,512]{3,2,1,0:T(8,128)(2,1)} %constant_dynamic-update-slice_fusion.o_ref, f32[1,8,1,512]{3,2,1,0:T(1,128)} %pad_maximum_fusion.19.lse_ref, ...), custom_call_target="tpu_custom_call" | custom-call | flops 42949672960 | bytes 8388608 | tf_op jit(solution)/shard_map/attention_backward/pallas_call | solution.py:251
  567.0 5.1 all-to-all-start.9
  581.3 4.5 fusion.69
  585.9 4.7 fusion.70
  590.5 16.1 %all-to-all-done.9 = bf16[8,3,64,512]{3,2,1,0:T(8,128)(2,1)} async-done(((bf16[8,3,64,512]{3,2,1,0:T(8,128)(2,1)}), bf16[8,3,64,512]{3,2,1,0:T(8,128)(2,1)}, u32[]{:S(2)}, u32[]{:S(2)}) %all-to-all-start.9) | async-done | bytes 1572896 | tf_op jit(solution)/shard_map/all_to_all | solution.py:282
  606.7 6.5 multiply_reduce_fusion.1
  636.2 4.3 add_convert_fusion
  651.3 5.2 all-to-all-start.10
  668.2 12.5 %multiply_convert_fusion = bf16[2,512,4416]{1,2,0:T(8,128)(2,1)} fusion(bf16[2,512,768]{2,1,0:T(8,128)(2,1)S(1)} %copy-done.36, f32[2,4416]{1,0:T(2,128)S(1)} %mul.445, bf16[4416,768]{1,0:T(8,128)(2,1)} %bitcast.27), kind=kOutput, calls=%fused_computation.1 | convolution fusion | flops 6954811392 | bytes 17435136 | tf_op jit(solution)/shard_map/fsd,pd->fsp/dot_general | solution.py:1035
  680.9 15.8 %collective-permute-done.48 = bf16[8,48,1664]{2,1,0:T(8,128)(2,1)S(1)} collective-permute-done((bf16[8,48,1664]{2,1,0:T(8,128)(2,1)S(1)}, bf16[8,48,1664]{2,1,0:T(8,128)(2,1)S(1)}, u32[]{:S(2)}, u32[]{:S(2)}) %collective-permute-start.48) | collective-permute-done | bytes 1277984 | tf_op jit(solution)/shard_map/ppermute | solution.py:311
  698.0 10.5 %all-to-all-done.10 = bf16[8,552,256]{2,1,0:T(8,128)(2,1)} async-done(((bf16[8,552,256]{2,1,0:T(8,128)(2,1)}), bf16[8,552,256]{2,1,0:T(8,128)(2,1)}, u32[]{:S(2)}, u32[]{:S(2)}) %all-to-all-start.10) | async-done | bytes 2261024 | tf_op jit(solution)/shard_map/all_to_all | solution.py:282
  718.6 26.6 %all-to-all-done.11 = bf16[8,48,1664]{2,1,0:T(8,128)(2,1)} async-done(((bf16[8,48,1664]{2,1,0:T(8,128)(2,1)}), bf16[8,48,1664]{2,1,0:T(8,128)(2,1)}, u32[]{:S(2)}, u32[]{:S(2)}) %all-to-all-start.11) | async-done | bytes 1277984 | tf_op jit(solution)/shard_map/all_to_all | solution.py:282
  747.8 4.3 collective-permute-done.49
  752.3 4.3 all-to-all-start.12
  759.6 25.2 %all-to-all-done.12 = bf16[8,552,128]{2,1,0:T(8,128)(2,1)S(1)} async-done(((bf16[8,552,128]{2,1,0:T(8,128)(2,1)}), bf16[8,552,128]{2,1,0:T(8,128)(2,1)S(1)}, u32[]{:S(2)}, u32[]{:S(2)}) %all-to-all-start.12) | async-done | bytes 1130528 | tf_op jit(solution)/shard_map/all_to_all | solution.py:282
  790.6 10.5 %collective-permute-done.56 = bf16[552,384]{1,0:T(8,128)(2,1)S(1)} collective-permute-done((bf16[552,384]{1,0:T(8,128)(2,1)S(1)}, bf16[552,384]{1,0:T(8,128)(2,1)S(1)}, u32[]{:S(2)}, u32[]{:S(2)}) %collective-permute-start.56) | collective-permute-done | bytes 423968 | tf_op jit(solution)/shard_map/ppermute | solution.py:311
  818.8 5.7 rest_finish.1
  (547 shorter events, 296.2 us)
Async XLA Ops:
  2.8 19.8 %collective-permute-start = (bf16[552,384]{1,0:T(8,128)(2,1)}, bf16[552,384]{1,0:T(8,128)(2,1)}, u32[]{:S(2)}, u32[]{:S(2)}) collective-permute-start(bf16[552,384]{1,0:T(8,128)(2,1)} %dynamic-slice_convert_fusion.1), channel_id=1, source_target_pairs={{0,1},{1,0},{2,3},{3,2},{4,5},{5,4},{6,7},{7,6},{8,9},{9,8},{10,11... | collective-permute-start | bytes 1271816 | tf_op jit(solution)/shard_map/ppermute | solution.py:300
  3.2 13.2 %collective-permute-start.1 = (bf16[552,384]{1,0:T(8,128)(2,1)}, bf16[552,384]{1,0:T(8,128)(2,1)}, u32[]{:S(2)}, u32[]{:S(2)}) collective-permute-start(bf16[552,384]{1,0:T(8,128)(2,1)} %dynamic-slice_convert_fusion.1), channel_id=1, source_target_pairs={{0,8},{8,16},{16,24},{24,28},{28,20},{20,12},{12,4},{4,0},{1,9},{9... | collective-permute-start | bytes 1271816 | tf_op jit(solution)/shard_map/ppermute | solution.py:378
  17.9 19.2 %collective-permute-start.5 = (bf16[552,384]{1,0:T(8,128)(2,1)}, bf16[552,384]{1,0:T(8,128)(2,1)S(1)}, u32[]{:S(2)}, u32[]{:S(2)}) collective-permute-start(bf16[552,384]{1,0:T(8,128)(2,1)} %collective-permute-done.1), channel_id=1, source_target_pairs={{0,8},{8,16},{16,24},{24,28},{28,20},{20,12},{12,4},{4,0},{1,9},{9... | collective-permute-start | bytes 1271816 | tf_op jit(solution)/shard_map/ppermute | solution.py:378
  19.5 17.6 %collective-permute-start.7 = (bf16[552,384]{1,0:T(8,128)(2,1)S(1)}, bf16[552,384]{1,0:T(8,128)(2,1)S(1)}, u32[]{:S(2)}, u32[]{:S(2)}) collective-permute-start(bf16[552,384]{1,0:T(8,128)(2,1)S(1)} %collective-permute-done.3), channel_id=1, source_target_pairs={{8,0},{16,8},{24,16},{28,24},{20,28},{12,20},{4,12},{0,4},{9,1},{1... | collective-permute-start | bytes 1271816 | tf_op jit(solution)/shard_map/ppermute | solution.py:378
  20.0 17.0 %collective-permute-start.13 = (bf16[1,96,512]{1,2,0:T(8,128)(2,1)S(1)}, bf16[1,96,512]{1,2,0:T(8,128)(2,1)S(1)}, u32[]{:S(2)}, u32[]{:S(2)}) collective-permute-start(bf16[1,96,512]{1,2,0:T(8,128)(2,1)S(1)} %fusion.114), channel_id=1, source_target_pairs={{0,16},{4,20},{8,24},{12,28},{16,0},{20,4},{24,8},{28,12},{1,17},{... | collective-permute-start | bytes 294920 | tf_op jit(solution)/shard_map/ppermute | solution.py:325
  22.6 16.7 %collective-permute-start.2 = (bf16[552,384]{1,0:T(8,128)(2,1)}, bf16[552,384]{1,0:T(8,128)(2,1)S(1)}, u32[]{:S(2)}, u32[]{:S(2)}) collective-permute-start(bf16[552,384]{1,0:T(8,128)(2,1)} %collective-permute-done.1), channel_id=1, source_target_pairs={{0,1},{1,0},{2,3},{3,2},{4,5},{5,4},{6,7},{7,6},{8,9},{9,8},{10,11... | collective-permute-start | bytes 1271816 | tf_op jit(solution)/shard_map/ppermute | solution.py:300
  22.6 19.4 %collective-permute-start.4 = (bf16[552,384]{1,0:T(8,128)(2,1)S(1)}, bf16[552,384]{1,0:T(8,128)(2,1)S(1)}, u32[]{:S(2)}, u32[]{:S(2)}) collective-permute-start(bf16[552,384]{1,0:T(8,128)(2,1)S(1)} %collective-permute-done.3), channel_id=1, source_target_pairs={{0,1},{1,0},{2,3},{3,2},{4,5},{5,4},{6,7},{7,6},{8,9},{9,8},{10,11... | collective-permute-start | bytes 1271816 | tf_op jit(solution)/shard_map/ppermute | solution.py:300
  37.1 14.9 %collective-permute-start.9 = (bf16[552,384]{1,0:T(8,128)(2,1)S(1)}, bf16[552,384]{1,0:T(8,128)(2,1)S(1)}, u32[]{:S(2)}, u32[]{:S(2)}) collective-permute-start(bf16[552,384]{1,0:T(8,128)(2,1)S(1)} %collective-permute-done.5), channel_id=1, source_target_pairs={{0,8},{8,16},{16,24},{24,28},{28,20},{20,12},{12,4},{4,0},{1,9},{9... | collective-permute-start | bytes 1271816 | tf_op jit(solution)/shard_map/ppermute | solution.py:378
  37.2 14.9 %collective-permute-start.11 = (bf16[552,384]{1,0:T(8,128)(2,1)S(1)}, bf16[552,384]{1,0:T(8,128)(2,1)S(1)}, u32[]{:S(2)}, u32[]{:S(2)}) collective-permute-start(bf16[552,384]{1,0:T(8,128)(2,1)S(1)} %collective-permute-done.7), channel_id=1, source_target_pairs={{8,0},{16,8},{24,16},{28,24},{20,28},{12,20},{4,12},{0,4},{9,1},{1... | collective-permute-start | bytes 1271816 | tf_op jit(solution)/shard_map/ppermute | solution.py:378
  39.2 12.5 %collective-permute-start.18 = (bf16[2,96,512]{1,2,0:T(8,128)(2,1)S(1)}, bf16[2,96,512]{1,2,0:T(8,128)(2,1)S(1)}, u32[]{:S(2)}, u32[]{:S(2)}) collective-permute-start(bf16[2,96,512]{1,2,0:T(8,128)(2,1)S(1)} %maximum_bitcast_fusion.15), channel_id=1, source_target_pairs={{0,8},{4,12},{8,0},{12,4},{16,24},{20,28},{24,16},{28,20},{1,9},{5... | collective-permute-start | bytes 589832 | tf_op jit(solution)/shard_map/ppermute | solution.py:325
  39.3 16.1 %collective-permute-start.6 = (bf16[552,384]{1,0:T(8,128)(2,1)S(1)}, bf16[552,384]{1,0:T(8,128)(2,1)}, u32[]{:S(2)}, u32[]{:S(2)}) collective-permute-start(bf16[552,384]{1,0:T(8,128)(2,1)S(1)} %collective-permute-done.5), channel_id=1, source_target_pairs={{0,1},{1,0},{2,3},{3,2},{4,5},{5,4},{6,7},{7,6},{8,9},{9,8},{10,11... | collective-permute-start | bytes 1271816 | tf_op jit(solution)/shard_map/ppermute | solution.py:300
  41.9 16.1 %collective-permute-start.8 = (bf16[552,384]{1,0:T(8,128)(2,1)S(1)}, bf16[552,384]{1,0:T(8,128)(2,1)}, u32[]{:S(2)}, u32[]{:S(2)}) collective-permute-start(bf16[552,384]{1,0:T(8,128)(2,1)S(1)} %collective-permute-done.7), channel_id=1, source_target_pairs={{0,1},{1,0},{2,3},{3,2},{4,5},{5,4},{6,7},{7,6},{8,9},{9,8},{10,11... | collective-permute-start | bytes 1271816 | tf_op jit(solution)/shard_map/ppermute | solution.py:300
  54.3 15.6 %collective-permute-start.19 = (bf16[4,96,512]{2,1,0:T(8,128)(2,1)S(1)}, bf16[4,96,512]{2,1,0:T(8,128)(2,1)S(1)}, u32[]{:S(2)}, u32[]{:S(2)}) collective-permute-start(bf16[4,96,512]{2,1,0:T(8,128)(2,1)S(1)} %bitcast.416), channel_id=1, source_target_pairs={{0,4},{4,0},{8,12},{12,8},{16,20},{20,16},{24,28},{28,24},{1,5},{5... | collective-permute-start | bytes 1179656 | tf_op jit(solution)/shard_map/ppermute | solution.py:325
  84.9 21.6 %collective-permute-start.23 = (bf16[4,48,1152]{2,1,0:T(8,128)(2,1)}, bf16[4,48,1152]{2,1,0:T(8,128)(2,1)}, u32[]{:S(2)}, u32[]{:S(2)}) collective-permute-start(bf16[4,48,1152]{2,1,0:T(8,128)(2,1)} %bitcast.50), channel_id=1, source_target_pairs={{0,4},{4,0},{8,12},{12,8},{16,20},{20,16},{24,28},{28,24},{1,5},{5... | collective-permute-start | bytes 1327112 | tf_op jit(solution)/shard_map/ppermute | solution.py:325
  108.9 20.4 %collective-permute-start.24 = (bf16[8,48,1152]{2,1,0:T(8,128)(2,1)}, bf16[8,48,1152]{2,1,0:T(8,128)(2,1)}, u32[]{:S(2)}, u32[]{:S(2)}) collective-permute-start(bf16[8,48,1152]{2,1,0:T(8,128)(2,1)} %bitcast.56), channel_id=1, source_target_pairs={{0,2},{2,0},{1,3},{3,1},{4,6},{6,4},{5,7},{7,5},{8,10},{10,8},{9,1... | collective-permute-start | bytes 2654216 | tf_op jit(solution)/shard_map/ppermute | solution.py:311
  110.4 40.1 %all-to-all-start = ((bf16[8,3,64,512]{3,2,1,0:T(8,128)(2,1)}), bf16[8,3,64,512]{3,2,1,0:T(8,128)(2,1)}, u32[]{:S(2)}, u32[]{:S(2)}) async-start(bf16[8,3,64,512]{3,2,1,0:T(8,128)(2,1)} %bitcast.396), calls=%async_computation | async-start | bytes 3145728 | tf_op jit(solution)/shard_map/all_to_all | solution.py:282
  146.6 38.2 %collective-permute-start.26 = (bf16[48,3072]{1,0:T(8,128)(2,1)}, bf16[48,3072]{1,0:T(8,128)(2,1)}, u32[]{:S(2)}, u32[]{:S(2)}) collective-permute-start(bf16[48,3072]{1,0:T(8,128)(2,1)} %get-tuple-element.118), channel_id=1, source_target_pairs={{0,8},{8,16},{16,24},{24,28},{28,20},{20,12},{12,4},{4,0},{1,9},{9... | collective-permute-start | bytes 884744 | tf_op jit(solution)/shard_map/ppermute | solution.py:378
  147.2 37.6 %collective-permute-start.27 = (bf16[48,3072]{1,0:T(8,128)(2,1)}, bf16[48,3072]{1,0:T(8,128)(2,1)}, u32[]{:S(2)}, u32[]{:S(2)}) collective-permute-start(bf16[48,3072]{1,0:T(8,128)(2,1)} %get-tuple-element.118), channel_id=1, source_target_pairs={{8,0},{16,8},{24,16},{28,24},{20,28},{12,20},{4,12},{0,4},{9,1},{1... | collective-permute-start | bytes 884744 | tf_op jit(solution)/shard_map/ppermute | solution.py:378
  150.5 59.9 %all-to-all-start.1 = ((bf16[8,3,64,512]{3,2,1,0:T(8,128)(2,1)}), bf16[8,3,64,512]{3,2,1,0:T(8,128)(2,1)}, u32[]{:S(2)}, u32[]{:S(2)}) async-start(bf16[8,3,64,512]{3,2,1,0:T(8,128)(2,1)} %bitcast.398), calls=%async_computation.1 | async-start | bytes 3145728 | tf_op jit(solution)/shard_map/all_to_all | solution.py:282
  210.4 39.9 %all-to-all-start.2 = ((bf16[8,3,64,512]{3,2,1,0:T(8,128)(2,1)}), bf16[8,3,64,512]{3,2,1,0:T(8,128)(2,1)}, u32[]{:S(2)}, u32[]{:S(2)}) async-start(bf16[8,3,64,512]{3,2,1,0:T(8,128)(2,1)} %bitcast.397), calls=%async_computation.2 | async-start | bytes 3145728 | tf_op jit(solution)/shard_map/all_to_all | solution.py:282
  250.4 36.1 %all-to-all-start.3 = ((bf16[8,2,64,512]{3,2,1,0:T(8,128)(2,1)}), bf16[8,2,64,512]{3,2,1,0:T(8,128)(2,1)}, u32[]{:S(2)}, u32[]{:S(2)}) async-start(bf16[8,2,64,512]{3,2,1,0:T(8,128)(2,1)} %pad_maximum_fusion.7), calls=%async_computation.3 | async-start | bytes 2097152 | tf_op jit(solution)/shard_map/all_to_all | solution.py:282
  257.4 29.0 %collective-permute-start.34 = (bf16[8,48,1536]{2,1,0:T(8,128)(2,1)S(1)}, bf16[8,48,1536]{2,1,0:T(8,128)(2,1)}, u32[]{:S(2)}, u32[]{:S(2)}) collective-permute-start(bf16[8,48,1536]{2,1,0:T(8,128)(2,1)S(1)} %bitcast.399), channel_id=1, source_target_pairs={{0,2},{2,0},{1,3},{3,1},{4,6},{6,4},{5,7},{7,5},{8,10},{10,8},{9,1... | collective-permute-start | bytes 3538952 | tf_op jit(solution)/shard_map/ppermute | solution.py:311
  259.3 50.4 %collective-permute-start.35 = (bf16[8,48,1536]{2,1,0:T(8,128)(2,1)}, bf16[8,48,1536]{2,1,0:T(8,128)(2,1)}, u32[]{:S(2)}, u32[]{:S(2)}) collective-permute-start(bf16[8,48,1536]{2,1,0:T(8,128)(2,1)} %bitcast.86), channel_id=1, source_target_pairs={{0,2},{2,0},{1,3},{3,1},{4,6},{6,4},{5,7},{7,5},{8,10},{10,8},{9,1... | collective-permute-start | bytes 3538952 | tf_op jit(solution)/shard_map/ppermute | solution.py:311
  295.7 21.7 %all-to-all-start.4 = ((bf16[8,1,64,512]{3,2,1,0:T(8,128)(2,1)}), bf16[8,1,64,512]{3,2,1,0:T(8,128)(2,1)}, u32[]{:S(2)}, u32[]{:S(2)}) async-start(bf16[8,1,64,512]{3,2,1,0:T(8,128)(2,1)} %constant_dynamic-update-slice_fusion.o_ref), calls=%async_computation.4 | async-start | bytes 1048576 | tf_op jit(solution)/shard_map/all_to_all | solution.py:282
  313.2 24.5 %collective-permute-start.37 = (bf16[768,1536]{1,0:T(8,128)(2,1)}, bf16[768,1536]{1,0:T(8,128)(2,1)}, u32[]{:S(2)}, u32[]{:S(2)}) collective-permute-start(bf16[768,1536]{1,0:T(8,128)(2,1)} %bitcast.89), channel_id=1, source_target_pairs={{0,1},{1,0},{2,3},{3,2},{4,5},{5,4},{6,7},{7,6},{8,9},{9,8},{10,11... | collective-permute-start | bytes 7077896 | tf_op jit(solution)/shard_map/ppermute | solution.py:300
  316.5 16.0 %collective-permute-start.36 = (bf16[768,1536]{1,0:T(8,128)(2,1)}, bf16[768,1536]{1,0:T(8,128)(2,1)}, u32[]{:S(2)}, u32[]{:S(2)}) collective-permute-start(bf16[768,1536]{1,0:T(8,128)(2,1)} %bitcast.84), channel_id=1, source_target_pairs={{0,1},{1,0},{2,3},{3,2},{4,5},{5,4},{6,7},{7,6},{8,9},{9,8},{10,11... | collective-permute-start | bytes 7077896 | tf_op jit(solution)/shard_map/ppermute | solution.py:300
  357.3 31.7 %collective-permute-start.38 = (bf16[768,1536]{1,0:T(8,128)(2,1)}, bf16[768,1536]{1,0:T(8,128)(2,1)}, u32[]{:S(2)}, u32[]{:S(2)}) collective-permute-start(bf16[768,1536]{1,0:T(8,128)(2,1)} %bitcast_convert_fusion.1), channel_id=1, source_target_pairs={{0,1},{1,0},{2,3},{3,2},{4,5},{5,4},{6,7},{7,6},{8,9},{9,8},{10,11... | collective-permute-start | bytes 7077896 | tf_op jit(solution)/shard_map/ppermute | solution.py:300
  366.7 27.6 %collective-permute-start.39 = (bf16[768,1536]{1,0:T(8,128)(2,1)}, bf16[768,1536]{1,0:T(8,128)(2,1)}, u32[]{:S(2)}, u32[]{:S(2)}) collective-permute-start(bf16[768,1536]{1,0:T(8,128)(2,1)} %bitcast_convert_fusion), channel_id=1, source_target_pairs={{0,1},{1,0},{2,3},{3,2},{4,5},{5,4},{6,7},{7,6},{8,9},{9,8},{10,11... | collective-permute-start | bytes 7077896 | tf_op jit(solution)/shard_map/ppermute | solution.py:300
  381.8 21.4 %all-to-all-start.5 = ((bf16[8,1,64,512]{3,2,1,0:T(8,128)(2,1)}), bf16[8,1,64,512]{3,2,1,0:T(8,128)(2,1)}, u32[]{:S(2)}, u32[]{:S(2)}) async-start(bf16[8,1,64,512]{3,2,1,0:T(8,128)(2,1)} %slice_bitcast_fusion.1), calls=%async_computation.5 | async-start | bytes 1048576 | tf_op jit(solution)/shard_map/all_to_all | solution.py:282
  401.5 53.4 %collective-permute-start.40 = (bf16[8,48,3072]{2,1,0:T(8,128)(2,1)S(1)}, bf16[8,48,3072]{2,1,0:T(8,128)(2,1)}, u32[]{:S(2)}, u32[]{:S(2)}) collective-permute-start(bf16[8,48,3072]{2,1,0:T(8,128)(2,1)S(1)} %dynamic-slice_bitcast_fusion), channel_id=1, source_target_pairs={{0,2},{2,0},{1,3},{3,1},{4,6},{6,4},{5,7},{7,5},{8,10},{10,8},{9,1... | collective-permute-start | bytes 7077896 | tf_op jit(solution)/shard_map/ppermute | solution.py:311
  403.2 57.4 %all-to-all-start.7 = ((bf16[8,2,64,512]{3,2,1,0:T(8,128)(2,1)}), bf16[8,2,64,512]{3,2,1,0:T(8,128)(2,1)}, u32[]{:S(2)}, u32[]{:S(2)}) async-start(bf16[8,2,64,512]{3,2,1,0:T(8,128)(2,1)} %slice_bitcast_fusion), calls=%async_computation.7 | async-start | bytes 2097152 | tf_op jit(solution)/shard_map/all_to_all | solution.py:282
  458.6 58.2 %collective-permute-start.41 = (bf16[4,48,3072]{2,1,0:T(8,128)(2,1)}, bf16[4,48,3072]{2,1,0:T(8,128)(2,1)}, u32[]{:S(2)}, u32[]{:S(2)}) collective-permute-start(bf16[4,48,3072]{2,1,0:T(8,128)(2,1)} %dynamic-slice_bitcast_fusion.2), channel_id=1, source_target_pairs={{0,4},{4,0},{8,12},{12,8},{16,20},{20,16},{24,28},{28,24},{1,5},{5... | collective-permute-start | bytes 3538952 | tf_op jit(solution)/shard_map/ppermute | solution.py:325
  460.6 50.1 %all-to-all-start.6 = ((bf16[8,3,64,512]{3,2,1,0:T(8,128)(2,1)}), bf16[8,3,64,512]{3,2,1,0:T(8,128)(2,1)}, u32[]{:S(2)}, u32[]{:S(2)}) async-start(bf16[8,3,64,512]{3,2,1,0:T(8,128)(2,1)} %attention_backward.3), calls=%async_computation.6 | async-start | bytes 3145728 | tf_op jit(solution)/shard_map/all_to_all | solution.py:282
  510.8 56.2 %all-to-all-start.8 = ((bf16[8,3,64,512]{3,2,1,0:T(8,128)(2,1)}), bf16[8,3,64,512]{3,2,1,0:T(8,128)(2,1)}, u32[]{:S(2)}, u32[]{:S(2)}) async-start(bf16[8,3,64,512]{3,2,1,0:T(8,128)(2,1)} %attention_backward.4), calls=%async_computation.8 | async-start | bytes 3145728 | tf_op jit(solution)/shard_map/all_to_all | solution.py:282
  519.5 53.1 %collective-permute-start.42 = (bf16[2,48,3072]{2,1,0:T(8,128)(2,1)S(1)}, bf16[2,48,3072]{2,1,0:T(8,128)(2,1)}, u32[]{:S(2)}, u32[]{:S(2)}) collective-permute-start(bf16[2,48,3072]{2,1,0:T(8,128)(2,1)S(1)} %dynamic-slice_bitcast_fusion.3), channel_id=1, source_target_pairs={{0,8},{4,12},{8,0},{12,4},{16,24},{20,28},{24,16},{28,20},{1,9},{5... | collective-permute-start | bytes 1769480 | tf_op jit(solution)/shard_map/ppermute | solution.py:325
  567.0 39.6 %all-to-all-start.9 = ((bf16[8,3,64,512]{3,2,1,0:T(8,128)(2,1)}), bf16[8,3,64,512]{3,2,1,0:T(8,128)(2,1)}, u32[]{:S(2)}, u32[]{:S(2)}) async-start(bf16[8,3,64,512]{3,2,1,0:T(8,128)(2,1)} %attention_backward.5), calls=%async_computation.9 | async-start | bytes 3145728 | tf_op jit(solution)/shard_map/all_to_all | solution.py:282
  580.9 47.7 %collective-permute-start.45 = (bf16[768,1152]{0,1:T(8,128)(2,1)}, bf16[768,1152]{0,1:T(8,128)(2,1)}, u32[]{:S(2)}, u32[]{:S(2)}) collective-permute-start(bf16[768,1152]{0,1:T(8,128)(2,1)} %pad_maximum_fusion.5), channel_id=1, source_target_pairs={{0,1},{1,0},{2,3},{3,2},{4,5},{5,4},{6,7},{7,6},{8,9},{9,8},{10,11... | collective-permute-start | bytes 5308424 | tf_op jit(solution)/shard_map/ppermute | solution.py:300
  619.2 16.9 %collective-permute-start.43 = (bf16[4416,256]{1,0:T(8,128)(2,1)S(1)}, bf16[4416,256]{1,0:T(8,128)(2,1)S(1)}, u32[]{:S(2)}, u32[]{:S(2)}) collective-permute-start(bf16[4416,256]{1,0:T(8,128)(2,1)S(1)} %fusion.4), channel_id=1, source_target_pairs={{0,1},{1,0},{2,3},{3,2},{4,5},{5,4},{6,7},{7,6},{8,9},{9,8},{10,11... | collective-permute-start | bytes 6782984 | tf_op jit(solution)/shard_map/ppermute | solution.py:300
  641.0 73.8 %collective-permute-start.54 = (f32[1,768]{1,0:T(1,128)S(1)}, f32[1,768]{1,0:T(1,128)S(1)}, u32[]{:S(2)}, u32[]{:S(2)}) collective-permute-start(f32[1,768]{1,0:T(1,128)S(1)} %broadcast_in_dim.174), channel_id=1, source_target_pairs={{0,2},{2,0},{1,3},{3,1},{4,6},{6,4},{5,7},{7,5},{8,10},{10,8},{9,1... | collective-permute-start | bytes 9224 | tf_op jit(solution)/shard_map/ppermute | solution.py:311
  643.9 14.9 %collective-permute-start.51 = (bf16[1,48,3072]{2,1,0:T(8,128)(2,1)}, bf16[1,48,3072]{2,1,0:T(8,128)(2,1)S(1)}, u32[]{:S(2)}, u32[]{:S(2)}) collective-permute-start(bf16[1,48,3072]{2,1,0:T(8,128)(2,1)} %constant_dynamic-slice_fusion), channel_id=1, source_target_pairs={{0,16},{4,20},{8,24},{12,28},{16,0},{20,4},{24,8},{28,12},{1,17},{... | collective-permute-start | bytes 884744 | tf_op jit(solution)/shard_map/ppermute | solution.py:325
  651.3 57.2 %all-to-all-start.10 = ((bf16[8,552,256]{2,1,0:T(8,128)(2,1)}), bf16[8,552,256]{2,1,0:T(8,128)(2,1)}, u32[]{:S(2)}, u32[]{:S(2)}) async-start(bf16[8,552,256]{2,1,0:T(8,128)(2,1)} %bitcast.125), calls=%async_computation.10 | async-start | bytes 4521984 | tf_op jit(solution)/shard_map/all_to_all | solution.py:282
  658.8 21.9 %collective-permute-start.52 = (bf16[1,48,3072]{2,1,0:T(8,128)(2,1)S(1)}, bf16[1,48,3072]{2,1,0:T(8,128)(2,1)S(1)}, u32[]{:S(2)}, u32[]{:S(2)}) collective-permute-start(bf16[1,48,3072]{2,1,0:T(8,128)(2,1)S(1)} %add_convert_fusion.4), channel_id=1, source_target_pairs={{0,2},{2,0},{1,3},{3,1},{4,6},{6,4},{5,7},{7,5},{8,10},{10,8},{9,1... | collective-permute-start | bytes 884744 | tf_op jit(solution)/shard_map/ppermute | solution.py:311
  666.9 29.8 %collective-permute-start.48 = (bf16[8,48,1664]{2,1,0:T(8,128)(2,1)S(1)}, bf16[8,48,1664]{2,1,0:T(8,128)(2,1)S(1)}, u32[]{:S(2)}, u32[]{:S(2)}) collective-permute-start(bf16[8,48,1664]{2,1,0:T(8,128)(2,1)S(1)} %dynamic-slice_bitcast_fusion.1), channel_id=1, source_target_pairs={{0,2},{2,0},{1,3},{3,1},{4,6},{6,4},{5,7},{7,5},{8,10},{10,8},{9,1... | collective-permute-start | bytes 3833864 | tf_op jit(solution)/shard_map/ppermute | solution.py:311
  680.8 35.3 %collective-permute-start.53 = (bf16[96,3072]{1,0:T(8,128)(2,1)S(1)}, bf16[96,3072]{1,0:T(8,128)(2,1)}, u32[]{:S(2)}, u32[]{:S(2)}) collective-permute-start(bf16[96,3072]{1,0:T(8,128)(2,1)S(1)} %bitcast.409), channel_id=1, source_target_pairs={{0,1},{1,0},{2,3},{3,2},{4,5},{5,4},{6,7},{7,6},{8,9},{9,8},{10,11... | collective-permute-start | bytes 1769480 | tf_op jit(solution)/shard_map/ppermute | solution.py:300
  710.6 34.7 %all-to-all-start.11 = ((bf16[8,48,1664]{2,1,0:T(8,128)(2,1)}), bf16[8,48,1664]{2,1,0:T(8,128)(2,1)}, u32[]{:S(2)}, u32[]{:S(2)}) async-start(bf16[8,48,1664]{2,1,0:T(8,128)(2,1)} %fusion.34), calls=%async_computation.11 | async-start | bytes 2555904 | tf_op jit(solution)/shard_map/all_to_all | solution.py:282
  752.3 32.5 %all-to-all-start.12 = ((bf16[8,552,128]{2,1,0:T(8,128)(2,1)}), bf16[8,552,128]{2,1,0:T(8,128)(2,1)S(1)}, u32[]{:S(2)}, u32[]{:S(2)}) async-start(bf16[8,552,128]{2,1,0:T(8,128)(2,1)} %bitcast.420), calls=%async_computation.12 | async-start | bytes 2260992 | tf_op jit(solution)/shard_map/all_to_all | solution.py:282
  785.9 24.0 %all-to-all-start.13 = ((f32[8,26,768]{2,1,0:T(8,128)}), f32[8,26,768]{2,1,0:T(8,128)S(1)}, u32[]{:S(2)}, u32[]{:S(2)}) async-start(f32[8,26,768]{2,1,0:T(8,128)} %broadcast_in_dim.175), calls=%async_computation.13 | async-start | bytes 1572864 | tf_op jit(solution)/shard_map/all_to_all | solution.py:282
  810.0 16.0 %all-to-all-start.14 = ((f32[8,8,768]{2,1,0:T(8,128)}), f32[8,8,768]{2,1,0:T(8,128)S(1)}, u32[]{:S(2)}, u32[]{:S(2)}) async-start(f32[8,8,768]{2,1,0:T(8,128)} %get-tuple-element.166), calls=%async_computation.14 | async-start | bytes 393216 | tf_op jit(solution)/shard_map/all_to_all | solution.py:282
  (121 other events, 1625.7 us)
